TPU v7x, 512 devices: a whole 4x4x16 slice. The times are simulated.
512 devices in a mesh: particle: 64 (over z, y), fsdp: 8 (over x, core).
Axes of the slice: x: 4, y: 4, z: 16, core: 2. Of those that a mesh axis runs over, the one named last changes fastest.
Arguments:
- particles: float32 [64, 256, 2048], P('particle', 'fsdp'), may hold values from -4.4 to 4.4, as said below
- gradients: float32 [64, 256, 2048], P('particle', 'fsdp'), may hold values from -0.0008544922 to 0.0008544922
- first_moment: float32 [64, 256, 2048], P('particle', 'fsdp'), may hold values from -0.00030517578 to 0.00030517578
- second_moment: float32 [64, 256, 2048], P('particle', 'fsdp'), may hold values from 9.094947e-13 to 9.094947e-11
- spread: float32 [], replicated, may hold values from 0.06 to 0.2
Outputs:
- new_particles: float32 [64, 256, 2048], P('particle', 'fsdp')
- new_first: float32 [64, 256, 2048], P('particle', 'fsdp')
- new_second: float32 [64, 256, 2048], P('particle', 'fsdp')
- direction: float32 [64, 256, 2048], P('particle', 'fsdp')
Inputs may be any that keep to these rules, and one draw needn't show every extreme that they name: `particles`: Real-valued parameters of each particle.
All inputs are finite; a program needn't handle non-finite values.
Results may differ from a plain program's by a relative error of at most 0.00015.
Values sent between devices are 32-bit elements; how exact they have to be, the bound alone decides.
No kernel may reach another device: no remote copies, remote signals or barrier semaphores. Data moves between devices by JAX's collectives and lax.ppermute only.
A program may use at most 64 MiB of HBM per device.

v0:
```python
import jax
import jax.numpy as jnp
from jax import lax
from jax.sharding import PartitionSpec as P

ADAM_STEP = 10


beta_one = 0.9
beta_two = 0.999
learn_rate = 0.05
adam_eps = 1e-08


def partial_gram(slab):
    return jnp.dot(
        slab, slab.T, precision=lax.Precision.HIGHEST, preferred_element_type=jnp.float32
    )


def body(particles, gradients, first_moment, second_moment, spread):
    count = lax.axis_size("particle")
    rows = particles.shape[1]
    cols = particles.shape[2]
    length = rows * cols // count
    total = rows * cols * lax.axis_size("fsdp")
    flat_x = particles.reshape(count, length)
    flat_g = gradients.reshape(count, length)
    slab_x, slab_g = (
        lax.all_to_all(flat_x, "particle", split_axis=0, concat_axis=0, tiled=True),
        lax.all_to_all(flat_g, "particle", split_axis=0, concat_axis=0, tiled=True),
    )
    local_gram = partial_gram(slab_x)
    gram = lax.psum(local_gram, ("particle", "fsdp"))
    diag = jnp.diagonal(gram)
    dist = diag[:, None] + diag[None, :] - 2.0 * gram
    kernel = jnp.exp(-dist / (spread * total))
    rowsum = jnp.sum(kernel, axis=1)
    pulled = jnp.dot(
        kernel, slab_g, precision=lax.Precision.HIGHEST, preferred_element_type=jnp.float32
    )
    kernel_x = jnp.dot(
        kernel, slab_x, precision=lax.Precision.HIGHEST, preferred_element_type=jnp.float32
    )
    push = 2.0 / (spread * total) * (rowsum[:, None] * slab_x - kernel_x)
    slab_dir = (pulled + push) / count
    direction = lax.all_to_all(
        slab_dir, "particle", split_axis=0, concat_axis=0, tiled=True
    ).reshape(particles.shape)
    new_first = beta_one * first_moment + (1.0 - beta_one) * direction
    new_second = beta_two * second_moment + (1.0 - beta_two) * direction * direction
    first_hat = new_first / (1.0 - beta_one**ADAM_STEP)
    second_hat = new_second / (1.0 - beta_two**ADAM_STEP)
    new_params = particles + learn_rate * first_hat / (jnp.sqrt(second_hat) + adam_eps)
    return (new_params, new_first, new_second, direction)


def solution(mesh):
    placed = (
        P("particle", "fsdp", None),
        P("particle", "fsdp", None),
        P("particle", "fsdp", None),
        P("particle", "fsdp", None),
        P(),
    )
    return jax.shard_map(
        body,
        mesh=mesh,
        in_specs=placed,
        out_specs=(
            P("particle", "fsdp", None),
            P("particle", "fsdp", None),
            P("particle", "fsdp", None),
            P("particle", "fsdp", None),
        ),
        check_vma=False,
    )
```

profile of v0, /device:TPU:1, one launch (start us, length us, event | category | flops | bytes accessed | tf_op | source)
XLA Modules:
  0.0 189.8 jit_solution(10178921238516675203)
XLA Ops:
  0.6 2.0 %all_to_all.22 = f32[64,1,1024]{2,1,0:T(1,128)} reshape(f32[1,32,2048]{2,1,0:T(8,128)} %param.5) | data formatting | bytes 524288 | tf_op jit(solution)/shard_map/all_to_all | solution.py:30
  2.6 0.0 copy-start.4
  2.6 19.4 %all-to-all-start = ((f32[64,1,1024]{2,1,0:T(1,128)}), f32[64,1,1024]{2,1,0:T(1,128)S(1)}, u32[]{:S(2)}, u32[]{:S(2)}) async-start(f32[64,1,1024]{2,1,0:T(1,128)} %all_to_all.22), calls=%async_computation | async-start | bytes 524288 | tf_op jit(solution)/shard_map/all_to_all | solution.py:30
  22.0 0.0 copy-done.4
  22.0 1.0 all_to_all.25
  23.0 18.2 %all-to-all-done = f32[64,1,1024]{2,1,0:T(1,128)S(1)} async-done(((f32[64,1,1024]{2,1,0:T(1,128)}), f32[64,1,1024]{2,1,0:T(1,128)S(1)}, u32[]{:S(2)}, u32[]{:S(2)}) %all-to-all-start) | async-done | bytes 262176 | tf_op jit(solution)/shard_map/all_to_all | solution.py:30
  41.2 7.4 %all-to-all-start.1 = ((f32[64,1,1024]{2,1,0:T(1,128)}), f32[64,1,1024]{2,1,0:T(1,128)S(1)}, u32[]{:S(2)}, u32[]{:S(2)}) async-start(f32[64,1,1024]{2,1,0:T(1,128)} %all_to_all.25), calls=%async_computation.1 | async-start | bytes 524288 | tf_op jit(solution)/shard_map/all_to_all | solution.py:31
  49.3 0.4 fusion.9
  49.7 105.6 %psum.7 = f32[64,64]{1,0:T(8,128)S(1)} all-reduce(f32[64,64]{1,0:T(8,128)S(1)} %fusion.9), channel_id=1, replica_groups=mesh['particle'=64,'fsdp'=8] {'particle','fsdp'}, use_global_device_ids=true, to_apply=%region_0.0 | all-reduce | flops 4096 | bytes 32768 | tf_op jit(solution)/shard_map/psum | solution.py:34
  155.3 0.8 gather_fusion
  156.1 0.2 fusion.13
  156.3 0.0 all-to-all-done.1
  156.3 0.4 fusion.5
  156.7 0.5 fusion.3
  157.2 0.3 copy.9
  157.5 29.6 %all_to_all.33 = f32[64,1,1024]{2,1,0:T(1,128)S(1)} all-to-all(f32[64,1,1024]{2,1,0:T(1,128)S(1)} %copy.9), channel_id=1, replica_groups=mesh['particle'=64,'fsdp'=8] {'particle'}, dimensions={0} | all-to-all | bytes 524288 | tf_op jit(solution)/shard_map/all_to_all | solution.py:47
  187.1 0.0 copy-start.3
  187.1 0.6 reduce
  187.7 0.0 copy-start
  187.7 0.0 copy-start.2
  187.7 0.1 reshape.64
  187.8 0.2 copy-done.3
  188.1 0.6 copy-done
  188.7 0.1 copy-done.2
  188.8 0.0 copy-start.1
  188.8 1.0 divide_add_fusion
  189.8 0.0 copy-done.1
  (1 shorter events, 0.0 us)
Async XLA Ops:
  2.6 19.4 %copy-start.4 = (f32[1,32,2048]{2,1,0:T(8,128)S(1)}, f32[1,32,2048]{2,1,0:T(8,128)}, u32[]{:S(2)}) copy-start(f32[1,32,2048]{2,1,0:T(8,128)} %param.6) | copy-start | bytes 786436
  2.6 38.6 %all-to-all-start = ((f32[64,1,1024]{2,1,0:T(1,128)}), f32[64,1,1024]{2,1,0:T(1,128)S(1)}, u32[]{:S(2)}, u32[]{:S(2)}) async-start(f32[64,1,1024]{2,1,0:T(1,128)} %all_to_all.22), calls=%async_computation | async-start | bytes 524288 | tf_op jit(solution)/shard_map/all_to_all | solution.py:30
  41.2 115.1 %all-to-all-start.1 = ((f32[64,1,1024]{2,1,0:T(1,128)}), f32[64,1,1024]{2,1,0:T(1,128)S(1)}, u32[]{:S(2)}, u32[]{:S(2)}) async-start(f32[64,1,1024]{2,1,0:T(1,128)} %all_to_all.25), calls=%async_computation.1 | async-start | bytes 524288 | tf_op jit(solution)/shard_map/all_to_all | solution.py:31
  187.1 1.0 copy-start.3
  187.7 1.0 copy-start
  187.7 1.0 copy-start.2
  188.8 1.0 copy-start.1
where the time goes:
time: 192 us; the launch traced here: 190 us
  blocking collectives  135 us (70%)
  starting transfers between devices  26.8 us (14%)
  waiting for transfers between devices  18.2 us (9%)
  local copies, waits for them, and re-layouts  5.09 us (3%)
    psum x1, blocking collectives, body(): gram = lax.psum(local_gram, ('particle', 'fsdp'))  106 us
    all_to_all x1, blocking collectives, body(): lax.all_to_all(slab_dir, 'particle', split_axis=0, concat_axis=0, tiled=T...  29.6 us
    all_to_all x1, starting transfers between devices, body(): lax.all_to_all(flat_x, 'particle', split_axis=0, concat_axis=0, tiled=True)  19.4 us
    all_to_all x1, waiting for transfers between devices, body(): lax.all_to_all(flat_x, 'particle', split_axis=0, concat_axis=0, tiled=True)  18.2 us
    all_to_all x1, starting transfers between devices, body(): lax.all_to_all(flat_g, 'particle', split_axis=0, concat_axis=0, tiled=True)  7.36 us
  transfers between devices with their start and end apart: 2, of which 1 were waited for; matrix products, arithmetic and copies ran while one was open for 1% of the time, Pallas kernels for 0%

commit v1 on v0

v1 whole, which is shorter than its diff:
```python
import functools

import jax
import jax.numpy as jnp
from jax import lax
from jax.experimental import pallas as pl
from jax.experimental.pallas import tpu as pltpu
from jax.sharding import Mesh, PartitionSpec as P

ADAM_STEP = 10

beta_one = 0.9
beta_two = 0.999
learn_rate = 0.05
adam_eps = 1e-08

COUNT = 64
HALF = COUNT // 2
SUB, LANE = 8, 128
PACK = 16

PLANE = ("y", "x", "core")
RING = ("z", "y")


def dot(a, b, dims):
    return lax.dot_general(
        a, b, (dims, ((), ())),
        precision=lax.Precision.HIGHEST, preferred_element_type=jnp.float32,
    )


def iota(shape, dim):
    return lax.broadcasted_iota(jnp.int32, shape, dim)


def dist_kernel(slab_ref, out_ref):
    x = jnp.concatenate([slab_ref[:, s, :] for s in range(SUB)], axis=1)
    gram = dot(x, jnp.concatenate([x, x], axis=0), ((1,), (1,)))
    lane = lax.rem(iota((COUNT, LANE), 1), COUNT)
    on_diag = jnp.where(lane == iota((COUNT, LANE), 0), gram, 0.0)
    norm_row = jnp.sum(on_diag, axis=0, keepdims=True)
    norm_col = 0.5 * jnp.sum(on_diag, axis=1, keepdims=True)
    dist = norm_col + norm_row - 2.0 * gram
    top = dist[:HALF]
    low = pltpu.roll(dist[HALF:], LANE - HALF, 1)
    lane = lax.rem(iota((HALF, LANE), 1), COUNT)
    keep = lane > iota((HALF, LANE), 0)
    both = jnp.where(keep, top, low)
    packed = jnp.where(iota((PACK, LANE), 1) < COUNT, both[:PACK], both[PACK:])
    for k in range(out_ref.shape[0]):
        out_ref[k] = packed


def sum_kernel(in_ref, out_ref):
    total = jnp.sum(in_ref[...], axis=0)
    for k in range(out_ref.shape[0]):
        out_ref[k] = total


def mix_kernel(entries, spread_ref, dist_ref, slab_ref, out_ref):
    packed = jnp.sum(dist_ref[...], axis=0)
    width = spread_ref[0] * entries
    packed = jnp.exp(-packed / width)
    both = jnp.concatenate([packed, pltpu.roll(packed, COUNT, 1)], axis=0)
    lane, row = iota((HALF, LANE), 1), iota((HALF, LANE), 0)
    top = jnp.where((lane > row) & (lane < COUNT), both, 0.0)
    low = jnp.where((lane >= HALF) & (lane - HALF < row), pltpu.roll(both, HALF, 1), 0.0)
    half = jnp.concatenate([top, low, jnp.zeros((LANE - COUNT, LANE), jnp.float32)], axis=0)
    eye = jnp.where(iota((LANE, LANE), 0) == iota((LANE, LANE), 1), 1.0, 0.0)
    kernel = (half + half.T + eye)[:COUNT, :COUNT]
    rowsum = jnp.sum(kernel, axis=1, keepdims=True)
    pull = 2.0 / jnp.full((COUNT, 1), width, jnp.float32)
    own = pull * rowsum
    x = jnp.concatenate([slab_ref[:, s, :] for s in range(SUB)], axis=1)
    g = jnp.concatenate([slab_ref[:, SUB + s, :] for s in range(SUB)], axis=1)
    mixed = dot(kernel, g - pull * x, ((1,), (0,)))
    mixed = (mixed + own * x) * (1.0 / COUNT)
    for s in range(SUB):
        out_ref[:, s, :] = mixed[:, s * LANE:(s + 1) * LANE]


def whole(count):
    return [pl.BlockSpec(memory_space=pltpu.VMEM)] * count


def tiles(block):
    rows, cols = block.shape
    return (
        block.reshape(rows // SUB, SUB, cols // LANE, LANE)
        .transpose(0, 2, 1, 3)
        .reshape(-1, SUB, LANE)
    )


def untiles(parts, rows, cols):
    return (
        parts.reshape(rows // SUB, cols // LANE, SUB, LANE)
        .transpose(0, 2, 1, 3)
        .reshape(rows, cols)
    )


def exchange(array, axes):
    return lax.all_to_all(array, axes, split_axis=0, concat_axis=0, tiled=True)


def body(particles, gradients, first_moment, second_moment, spread):
    _, rows, cols = particles.shape
    entries = rows * cols * lax.axis_size("x") * lax.axis_size("core")
    plane = lax.axis_size("y") * lax.axis_size("x") * lax.axis_size("core")
    depth = lax.axis_size("z")
    with jax.named_scope("gather_slab"):
        both = jnp.concatenate([tiles(particles[0]), tiles(gradients[0])], axis=1)
        slab = exchange(both, RING)
    with jax.named_scope("distances"):
        part = pl.pallas_call(
            dist_kernel,
            out_shape=jax.ShapeDtypeStruct((plane, PACK, LANE), jnp.float32),
            in_specs=whole(1),
            out_specs=whole(1)[0],
        )(slab)
        part = exchange(part, PLANE)
        part = pl.pallas_call(
            sum_kernel,
            out_shape=jax.ShapeDtypeStruct((depth, PACK, LANE), jnp.float32),
            in_specs=whole(1),
            out_specs=whole(1)[0],
        )(part)
        part = exchange(part, "z")
    with jax.named_scope("mix"):
        mixed = pl.pallas_call(
            functools.partial(mix_kernel, float(entries)),
            out_shape=jax.ShapeDtypeStruct((COUNT, SUB, LANE), jnp.float32),
            in_specs=[pl.BlockSpec(memory_space=pltpu.SMEM)] + whole(2),
            out_specs=whole(1)[0],
        )(spread.reshape(1), part, slab)
    with jax.named_scope("return_slab"):
        direction = untiles(exchange(mixed, RING), rows, cols)[None]
    with jax.named_scope("adam"):
        new_first = beta_one * first_moment + (1.0 - beta_one) * direction
        new_second = beta_two * second_moment + (1.0 - beta_two) * direction * direction
        first_hat = new_first / (1.0 - beta_one**ADAM_STEP)
        second_hat = new_second / (1.0 - beta_two**ADAM_STEP)
        new_params = particles + learn_rate * first_hat / (jnp.sqrt(second_hat) + adam_eps)
    return (new_params, new_first, new_second, direction)


def solution(mesh):
    split = Mesh(mesh.devices.reshape(16, 4, 4, 2), ("z", "y", "x", "core"))
    block = P(("z", "y"), ("x", "core"), None)
    return jax.shard_map(
        body,
        mesh=split,
        in_specs=(block, block, block, block, P()),
        out_specs=(block, block, block, block),
        check_vma=False,
    )
```

time: 192 us -> 125 us (0.65)
  blocking collectives: 135 us -> 96.6 us
  starting transfers between devices: 26.8 us -> 3.51 us
  Pallas kernels: 0 us -> 6.86 us
  waiting for transfers between devices: 18.2 us -> 11.7 us
  local copies, waits for them, and re-layouts: 5.09 us -> 1.37 us
    psum x1 -> x0, blocking collectives: 106 us -> none  [body(): gram = lax.psum(local_gram, ('particle', 'fsdp'))]
    all_to_all x1 -> x3, blocking collectives: 29.6 us -> 96.6 us  [exchange(): return lax.all_to_all(array, axes, split_axis=0, concat_axis=0, tiled=True)]
    all_to_all x2 -> x1, starting transfers between devices: 26.8 us -> 3.51 us  [exchange(): return lax.all_to_all(array, axes, split_axis=0, concat_axis=0, tiled=True)]
    pallas_call x0 -> x3, Pallas kernels: none -> 6.86 us  [the longest x1 2.61 us: body(): pl.pallas_call(dist_kernel, out_shape=jax.ShapeDtypeStruct((plane, PACK,...]
    all_to_all x2 -> x1, waiting for transfers between devices: 18.2 us -> 11.7 us  [exchange(): return lax.all_to_all(array, axes, split_axis=0, concat_axis=0, tiled=True)]
    all_to_all x3 -> x0, local copies, waits for them, and re-layouts: 3.25 us -> none  [the longest x1 1.96 us: body(): lax.all_to_all(flat_x, 'particle', split_axis=0, concat_axis=0, tiled=True)]
  transfers between devices with their start and end apart: 2 -> 1, of which waited for: 1 -> 1; matrix products, arithmetic and copies ran while one was open for 1% -> 0% of each run, Pallas kernels for 0% -> 0%
where the time goes in v1:
time: 125 us; the launch traced here: 123 us
  blocking collectives  96.6 us (77%)
  waiting for transfers between devices  11.7 us (9%)
  Pallas kernels  6.86 us (5%)
  starting transfers between devices  3.51 us (3%)
  other arithmetic  2.04 us (2%)
  local copies, waits for them, and re-layouts  1.37 us (1%)
  between operations  1.3 us (1%)
    all_to_all x3, blocking collectives, exchange(): return lax.all_to_all(array, axes, split_axis=0, concat_axis=0, tiled=True)  96.6 us
    all_to_all x1, waiting for transfers between devices, exchange(): return lax.all_to_all(array, axes, split_axis=0, concat_axis=0, tiled=True)  11.7 us
    all_to_all x1, starting transfers between devices, exchange(): return lax.all_to_all(array, axes, split_axis=0, concat_axis=0, tiled=True)  3.51 us
    pallas_call x1, Pallas kernels, body(): pl.pallas_call(dist_kernel, out_shape=jax.ShapeDtypeStruct((plane, PACK,...  2.61 us
    pallas_call x1, Pallas kernels, body(): pl.pallas_call(functools.partial(mix_kernel, float(entries)), out_shape=j...  2.6 us
  transfers between devices with their start and end apart: 1, of which 1 were waited for; matrix products, arithmetic and copies ran while one was open for 0% of the time, Pallas kernels for 0%

profile of v1, /device:TPU:1, one launch (start us, length us, event | category | flops | bytes accessed | tf_op | source)
XLA Modules:
  0.0 123.4 jit_solution(7524162369608785565)
XLA Ops:
  0.6 1.1 pad_maximum_fusion
  1.7 49.2 %all_to_all.20.slab_ref = f32[64,16,128]{2,1,0:T(8,128)} all-to-all(f32[64,16,128]{2,1,0:T(8,128)S(1)} %pad_maximum_fusion), channel_id=1, replica_groups=mesh['z'=16,'y'=4,'x'=4,'core'=2] {'z','y'}, dimensions={0} | all-to-all | bytes 1048576 | tf_op jit(solution)/shard_map/gather_slab/all_to_all | solution.py:105
  50.9 2.6 %distances.2 = f32[32,16,128]{2,1,0:T(8,128)} custom-call(f32[64,16,128]{2,1,0:T(8,128)} %all_to_all.20.slab_ref), custom_call_target="tpu_custom_call" | custom-call | tf_op jit(solution)/shard_map/distances/pallas_call | solution.py:117
  53.5 19.6 %all_to_all.21.in_ref = f32[32,16,128]{2,1,0:T(8,128)} all-to-all(f32[32,16,128]{2,1,0:T(8,128)} %distances.2), channel_id=1, replica_groups=mesh['z'=16,'y'=4,'x'=4,'core'=2] {'y','x','core'}, dimensions={0} | all-to-all | bytes 524288 | tf_op jit(solution)/shard_map/distances/all_to_all | solution.py:105
  73.1 1.6 %distances.3 = f32[16,16,128]{2,1,0:T(8,128)} custom-call(f32[32,16,128]{2,1,0:T(8,128)} %all_to_all.21.in_ref), custom_call_target="tpu_custom_call" | custom-call | tf_op jit(solution)/shard_map/distances/pallas_call | solution.py:124
  74.8 3.5 %all-to-all-start.2 = ((f32[16,16,128]{2,1,0:T(8,128)}), f32[16,16,128]{2,1,0:T(8,128)S(1)}, u32[]{:S(2)}, u32[]{:S(2)}) async-start(f32[16,16,128]{2,1,0:T(8,128)} %distances.3), calls=%async_computation.2 | async-start | bytes 262144 | tf_op jit(solution)/shard_map/distances/all_to_all | solution.py:105
  79.0 11.7 %all-to-all-done.2.dist_ref = f32[16,16,128]{2,1,0:T(8,128)S(1)} async-done(((f32[16,16,128]{2,1,0:T(8,128)}), f32[16,16,128]{2,1,0:T(8,128)S(1)}, u32[]{:S(2)}, u32[]{:S(2)}) %all-to-all-start.2) | async-done | bytes 131104 | tf_op jit(solution)/shard_map/distances/all_to_all | solution.py:105
  90.7 0.0 copy-start.1
  90.7 0.7 copy-done.1
  91.3 0.0 copy-start.3
  91.3 2.6 %mix.1 = f32[64,8,128]{2,1,0:T(8,128)} custom-call(f32[1]{0:T(128)} %bitcast.18.spread_ref, f32[16,16,128]{2,1,0:T(8,128)} %copy-done.1, f32[64,16,128]{2,1,0:T(8,128)} %all_to_all.20.slab_ref), custom_call_target="tpu_custom_call" | custom-call | tf_op jit(solution)/shard_map/mix/pallas_call | solution.py:132
  94.0 0.0 copy-start
  94.0 0.0 copy-start.2
  94.0 27.8 %all_to_all.22 = f32[64,8,128]{2,1,0:T(8,128)S(1)} all-to-all(f32[64,8,128]{2,1,0:T(8,128)} %mix.1), channel_id=1, replica_groups=mesh['z'=16,'y'=4,'x'=4,'core'=2] {'z','y'}, dimensions={0} | all-to-all | bytes 524288 | tf_op jit(solution)/shard_map/return_slab/all_to_all | solution.py:105
  121.7 0.0 copy-done.3
  121.7 0.0 copy-done
  121.7 0.0 copy-done.2
  121.7 1.0 divide_add_fusion
  122.7 0.7 copy.11
Async XLA Ops:
  74.8 15.9 %all-to-all-start.2 = ((f32[16,16,128]{2,1,0:T(8,128)}), f32[16,16,128]{2,1,0:T(8,128)S(1)}, u32[]{:S(2)}, u32[]{:S(2)}) async-start(f32[16,16,128]{2,1,0:T(8,128)} %distances.3), calls=%async_computation.2 | async-start | bytes 262144 | tf_op jit(solution)/shard_map/distances/all_to_all | solution.py:105
  90.7 0.7 copy-start.1
  91.3 30.4 %copy-start.3 = (f32[1,32,2048]{2,1,0:T(8,128)S(1)}, f32[1,32,2048]{2,1,0:T(8,128)}, u32[]{:S(2)}) copy-start(f32[1,32,2048]{2,1,0:T(8,128)} %param.8) | copy-start | bytes 786436
  94.0 27.8 %copy-start = (f32[1,32,2048]{2,1,0:T(8,128)S(1)}, f32[1,32,2048]{2,1,0:T(8,128)}, u32[]{:S(2)}) copy-start(f32[1,32,2048]{2,1,0:T(8,128)} %param.5) | copy-start | bytes 786436
  94.0 27.8 %copy-start.2 = (f32[1,32,2048]{2,1,0:T(8,128)S(1)}, f32[1,32,2048]{2,1,0:T(8,128)}, u32[]{:S(2)}) copy-start(f32[1,32,2048]{2,1,0:T(8,128)} %param.7) | copy-start | bytes 786436

commit v2 on v1

--- a/solution.py
+++ b/solution.py
@@ -1,5 +1,3 @@
-import functools
-
 import jax
 import jax.numpy as jnp
 from jax import lax
@@ -17,6 +15,7 @@
 COUNT = 64
 HALF = COUNT // 2
 SUB, LANE = 8, 128
+CHUNKS = 4
 PACK = 16
 
 PLANE = ("y", "x", "core")
@@ -32,6 +31,17 @@
 
 def iota(shape, dim):
     return lax.broadcasted_iota(jnp.int32, shape, dim)
+
+
+def stack_kernel(x_ref, g_ref, out_ref, sems):
+    copies = [
+        pltpu.make_async_copy(x_ref, out_ref.at[:, pl.ds(0, SUB), :], sems.at[0]),
+        pltpu.make_async_copy(g_ref, out_ref.at[:, pl.ds(SUB, SUB), :], sems.at[1]),
+    ]
+    for copy in copies:
+        copy.start()
+    for copy in copies:
+        copy.wait()
 
 
 def dist_kernel(slab_ref, out_ref):
@@ -58,10 +68,8 @@
         out_ref[k] = total
 
 
-def mix_kernel(entries, spread_ref, dist_ref, slab_ref, out_ref):
-    packed = jnp.sum(dist_ref[...], axis=0)
-    width = spread_ref[0] * entries
-    packed = jnp.exp(-packed / width)
+def mix_kernel(width_ref, dist_ref, slab_ref, out_ref):
+    packed = jnp.exp(-jnp.sum(dist_ref[...], axis=0) / width_ref[0:1])
     both = jnp.concatenate([packed, pltpu.roll(packed, COUNT, 1)], axis=0)
     lane, row = iota((HALF, LANE), 1), iota((HALF, LANE), 0)
     top = jnp.where((lane > row) & (lane < COUNT), both, 0.0)
@@ -70,7 +78,7 @@
     eye = jnp.where(iota((LANE, LANE), 0) == iota((LANE, LANE), 1), 1.0, 0.0)
     kernel = (half + half.T + eye)[:COUNT, :COUNT]
     rowsum = jnp.sum(kernel, axis=1, keepdims=True)
-    pull = 2.0 / jnp.full((COUNT, 1), width, jnp.float32)
+    pull = 2.0 / width_ref[0:1, 0:1]
     own = pull * rowsum
     x = jnp.concatenate([slab_ref[:, s, :] for s in range(SUB)], axis=1)
     g = jnp.concatenate([slab_ref[:, SUB + s, :] for s in range(SUB)], axis=1)
@@ -80,8 +88,44 @@
         out_ref[:, s, :] = mixed[:, s * LANE:(s + 1) * LANE]
 
 
-def whole(count):
-    return [pl.BlockSpec(memory_space=pltpu.VMEM)] * count
+def adam_kernel(x_ref, m_ref, v_ref, d_ref, new_x, new_m, new_v, new_d, out_x, out_m, out_v, sems):
+    copies = [pltpu.make_async_copy(d_ref, new_d, sems.at[0])]
+    copies[0].start()
+    rows = x_ref.shape[0] // CHUNKS
+    for k in range(CHUNKS):
+        part = pl.ds(k * rows, rows)
+        direction = d_ref[part]
+        first = beta_one * m_ref[part] + (1.0 - beta_one) * direction
+        second = beta_two * v_ref[part] + (1.0 - beta_two) * direction * direction
+        out_m[part] = first
+        out_v[part] = second
+        first_hat = first / (1.0 - beta_one**ADAM_STEP)
+        second_hat = second / (1.0 - beta_two**ADAM_STEP)
+        out_x[part] = x_ref[part] + learn_rate * first_hat / (jnp.sqrt(second_hat) + adam_eps)
+        for i, (src, dst) in enumerate(((out_m, new_m), (out_v, new_v), (out_x, new_x))):
+            copy = pltpu.make_async_copy(src.at[part], dst.at[part], sems.at[1 + 3 * k + i])
+            copy.start()
+            copies.append(copy)
+    for copy in copies:
+        copy.wait()
+
+
+IN_VMEM = pl.BlockSpec(memory_space=pltpu.VMEM)
+ANYWHERE = pl.BlockSpec(memory_space=pl.ANY)
+
+
+def call(kernel, out_shape, in_specs, args, out_specs=IN_VMEM, scratch=()):
+    args = [
+        pltpu.with_memory_space_constraint(a, pltpu.VMEM if s is IN_VMEM else pltpu.HBM)
+        for a, s in zip(args, in_specs)
+    ]
+    return pl.pallas_call(
+        kernel, out_shape=out_shape, in_specs=in_specs, out_specs=out_specs, scratch_shapes=list(scratch)
+    )(*args)
+
+
+def vmem(*shape):
+    return pltpu.VMEM(shape, jnp.float32)
 
 
 def tiles(block):
@@ -111,39 +155,31 @@
     plane = lax.axis_size("y") * lax.axis_size("x") * lax.axis_size("core")
     depth = lax.axis_size("z")
     with jax.named_scope("gather_slab"):
-        both = jnp.concatenate([tiles(particles[0]), tiles(gradients[0])], axis=1)
+        both = call(
+            stack_kernel, vmem(COUNT, 2 * SUB, LANE), [ANYWHERE] * 2,
+            (tiles(particles[0]), tiles(gradients[0])),
+            scratch=[pltpu.SemaphoreType.DMA((2,))],
+        )
         slab = exchange(both, RING)
     with jax.named_scope("distances"):
-        part = pl.pallas_call(
-            dist_kernel,
-            out_shape=jax.ShapeDtypeStruct((plane, PACK, LANE), jnp.float32),
-            in_specs=whole(1),
-            out_specs=whole(1)[0],
-        )(slab)
+        part = call(dist_kernel, vmem(plane, PACK, LANE), [IN_VMEM], (slab,))
         part = exchange(part, PLANE)
-        part = pl.pallas_call(
-            sum_kernel,
-            out_shape=jax.ShapeDtypeStruct((depth, PACK, LANE), jnp.float32),
-            in_specs=whole(1),
-            out_specs=whole(1)[0],
-        )(part)
+        part = call(sum_kernel, vmem(depth, PACK, LANE), [IN_VMEM], (part,))
         part = exchange(part, "z")
     with jax.named_scope("mix"):
-        mixed = pl.pallas_call(
-            functools.partial(mix_kernel, float(entries)),
-            out_shape=jax.ShapeDtypeStruct((COUNT, SUB, LANE), jnp.float32),
-            in_specs=[pl.BlockSpec(memory_space=pltpu.SMEM)] + whole(2),
-            out_specs=whole(1)[0],
-        )(spread.reshape(1), part, slab)
+        width = jnp.full((SUB, LANE), spread * entries, jnp.float32)
+        mixed = call(mix_kernel, vmem(COUNT, SUB, LANE), [IN_VMEM] * 3, (width, part, slab))
     with jax.named_scope("return_slab"):
-        direction = untiles(exchange(mixed, RING), rows, cols)[None]
+        direction = untiles(exchange(mixed, RING), rows, cols)
     with jax.named_scope("adam"):
-        new_first = beta_one * first_moment + (1.0 - beta_one) * direction
-        new_second = beta_two * second_moment + (1.0 - beta_two) * direction * direction
-        first_hat = new_first / (1.0 - beta_one**ADAM_STEP)
-        second_hat = new_second / (1.0 - beta_two**ADAM_STEP)
-        new_params = particles + learn_rate * first_hat / (jnp.sqrt(second_hat) + adam_eps)
-    return (new_params, new_first, new_second, direction)
+        block = jax.ShapeDtypeStruct((rows, cols), jnp.float32)
+        outs = call(
+            adam_kernel, (block,) * 4, [IN_VMEM] * 4,
+            (particles[0], first_moment[0], second_moment[0], direction),
+            out_specs=(ANYWHERE,) * 4,
+            scratch=[vmem(rows, cols)] * 3 + [pltpu.SemaphoreType.DMA((1 + 3 * CHUNKS,))],
+        )
+    return tuple(out[None] for out in outs)
 
 
 def solution(mesh):

time: 125 us -> 119 us (0.952)
  Pallas kernels: 6.86 us -> 4.46 us
  other arithmetic: 2.04 us -> 0 us
  local copies, waits for them, and re-layouts: 1.37 us -> 0.02 us
    pallas_call x3 -> x5, Pallas kernels: 6.86 us -> 4.46 us  [call(): pl.pallas_call(kernel, out_shape=out_shape, in_specs=in_specs, out_specs=...]
    unnamed x9 -> x6, local copies, waits for them, and re-layouts: 1.37 us -> 0.02 us
where the time goes in v2:
time: 119 us; the launch traced here: 117 us
  blocking collectives  96 us (81%)
  waiting for transfers between devices  11.7 us (10%)
  Pallas kernels  4.46 us (4%)
  starting transfers between devices  3.51 us (3%)
  between operations  1.33 us (1%)
    all_to_all x3, blocking collectives, exchange(): return lax.all_to_all(array, axes, split_axis=0, concat_axis=0, tiled=True)  96 us
    all_to_all x1, waiting for transfers between devices, exchange(): return lax.all_to_all(array, axes, split_axis=0, concat_axis=0, tiled=True)  11.7 us
    pallas_call x5, Pallas kernels, call(): pl.pallas_call(kernel, out_shape=out_shape, in_specs=in_specs, out_specs=...  4.46 us
    all_to_all x1, starting transfers between devices, exchange(): return lax.all_to_all(array, axes, split_axis=0, concat_axis=0, tiled=True)  3.51 us
  transfers between devices with their start and end apart: 1, of which 1 were waited for; matrix products, arithmetic and copies ran while one was open for 0% of the time, Pallas kernels for 0%

profile of v2, /device:TPU:1, one launch (start us, length us, event | category | flops | bytes accessed | tf_op | source)
XLA Modules:
  0.0 117.0 jit_solution(4552805178032449716)
XLA Ops:
  0.6 1.0 gather_slab.1
  1.7 49.1 %all_to_all.20.slab_ref = f32[64,16,128]{2,1,0:T(8,128)S(1)} all-to-all(f32[64,16,128]{2,1,0:T(8,128)S(1)} %gather_slab.1), channel_id=1, replica_groups=mesh['z'=16,'y'=4,'x'=4,'core'=2] {'z','y'}, dimensions={0} | all-to-all | bytes 1048576 | tf_op jit(solution)/shard_map/gather_slab/all_to_all | solution.py:149
  50.8 0.9 distances.2
  51.7 19.3 %all_to_all.21.in_ref = f32[32,16,128]{2,1,0:T(8,128)S(1)} all-to-all(f32[32,16,128]{2,1,0:T(8,128)S(1)} %distances.2), channel_id=1, replica_groups=mesh['z'=16,'y'=4,'x'=4,'core'=2] {'y','x','core'}, dimensions={0} | all-to-all | bytes 524288 | tf_op jit(solution)/shard_map/distances/all_to_all | solution.py:149
  71.0 0.7 distances.3
  71.7 3.5 %all-to-all-start.2 = ((f32[16,16,128]{2,1,0:T(8,128)}), f32[16,16,128]{2,1,0:T(8,128)S(1)}, u32[]{:S(2)}, u32[]{:S(2)}) async-start(f32[16,16,128]{2,1,0:T(8,128)} %distances.3), calls=%async_computation.2 | async-start | bytes 262144 | tf_op jit(solution)/shard_map/distances/all_to_all | solution.py:149
  75.9 11.7 %all-to-all-done.2.dist_ref = f32[16,16,128]{2,1,0:T(8,128)S(1)} async-done(((f32[16,16,128]{2,1,0:T(8,128)}), f32[16,16,128]{2,1,0:T(8,128)S(1)}, u32[]{:S(2)}, u32[]{:S(2)}) %all-to-all-start.2) | async-done | bytes 131104 | tf_op jit(solution)/shard_map/distances/all_to_all | solution.py:149
  87.6 0.0 copy-start.2
  87.6 0.8 mix.1
  88.4 0.0 copy-start
  88.4 0.0 copy-start.1
  88.4 27.6 %all_to_all.22 = f32[64,8,128]{2,1,0:T(8,128)S(1)} all-to-all(f32[64,8,128]{2,1,0:T(8,128)S(1)} %mix.1), channel_id=1, replica_groups=mesh['z'=16,'y'=4,'x'=4,'core'=2] {'z','y'}, dimensions={0} | all-to-all | bytes 524288 | tf_op jit(solution)/shard_map/return_slab/all_to_all | solution.py:149
  115.9 0.0 copy-done.2
  116.0 0.0 copy-done
  116.0 0.0 copy-done.1
  116.0 1.1 adam.1
  (1 shorter events, 0.0 us)
Async XLA Ops:
  71.7 15.9 %all-to-all-start.2 = ((f32[16,16,128]{2,1,0:T(8,128)}), f32[16,16,128]{2,1,0:T(8,128)S(1)}, u32[]{:S(2)}, u32[]{:S(2)}) async-start(f32[16,16,128]{2,1,0:T(8,128)} %distances.3), calls=%async_computation.2 | async-start | bytes 262144 | tf_op jit(solution)/shard_map/distances/all_to_all | solution.py:149
  87.6 28.4 %copy-start.2 = (f32[1,32,2048]{2,1,0:T(8,128)S(1)}, f32[1,32,2048]{2,1,0:T(8,128)}, u32[]{:S(2)}) copy-start(f32[1,32,2048]{2,1,0:T(8,128)} %param.8) | copy-start | bytes 786436
  88.4 27.6 %copy-start = (f32[1,32,2048]{2,1,0:T(8,128)S(1)}, f32[1,32,2048]{2,1,0:T(8,128)}, u32[]{:S(2)}) copy-start(f32[1,32,2048]{2,1,0:T(8,128)} %param.5) | copy-start | bytes 786436
  88.4 27.6 %copy-start.1 = (f32[1,32,2048]{2,1,0:T(8,128)S(1)}, f32[1,32,2048]{2,1,0:T(8,128)}, u32[]{:S(2)}) copy-start(f32[1,32,2048]{2,1,0:T(8,128)} %param.7) | copy-start | bytes 786436

commit v3 on v2

--- a/solution.py
+++ b/solution.py
@@ -17,8 +17,9 @@
 SUB, LANE = 8, 128
 CHUNKS = 4
 PACK = 16
-
-PLANE = ("y", "x", "core")
+PACKED = PACK // SUB
+
+PLANE = ("y", "x")
 RING = ("z", "y")
 
 
@@ -33,18 +34,9 @@
     return lax.broadcasted_iota(jnp.int32, shape, dim)
 
 
-def stack_kernel(x_ref, g_ref, out_ref, sems):
-    copies = [
-        pltpu.make_async_copy(x_ref, out_ref.at[:, pl.ds(0, SUB), :], sems.at[0]),
-        pltpu.make_async_copy(g_ref, out_ref.at[:, pl.ds(SUB, SUB), :], sems.at[1]),
-    ]
-    for copy in copies:
-        copy.start()
-    for copy in copies:
-        copy.wait()
-
-
-def dist_kernel(slab_ref, out_ref):
+def pack_kernel(width_ref, slab_ref, g_ref, out_ref, sem):
+    copy = pltpu.make_async_copy(g_ref, out_ref.at[pl.ds(PACKED, COUNT)], sem)
+    copy.start()
     x = jnp.concatenate([slab_ref[:, s, :] for s in range(SUB)], axis=1)
     gram = dot(x, jnp.concatenate([x, x], axis=0), ((1,), (1,)))
     lane = lax.rem(iota((COUNT, LANE), 1), COUNT)
@@ -57,9 +49,33 @@
     lane = lax.rem(iota((HALF, LANE), 1), COUNT)
     keep = lane > iota((HALF, LANE), 0)
     both = jnp.where(keep, top, low)
-    packed = jnp.where(iota((PACK, LANE), 1) < COUNT, both[:PACK], both[PACK:])
+    packed = jnp.where(iota((PACK, LANE), 1) < COUNT, both[:PACK], both[PACK:]) / width_ref[0:1]
+    for k in range(PACKED):
+        out_ref[k] = packed[k * SUB:(k + 1) * SUB]
+    copy.wait()
+
+
+def spread_kernel(both_ref, out_ref):
+    total = both_ref[0, 0:PACKED] + both_ref[1, 0:PACKED]
     for k in range(out_ref.shape[0]):
-        out_ref[k] = packed
+        out_ref[k] = total
+
+
+def stack_kernel(both_ref, out_ref):
+    out_ref[:, 0:SUB, :] = both_ref[0, PACKED:]
+    out_ref[:, SUB:, :] = both_ref[1, PACKED:]
+
+
+def last_kernel(in_ref, out_ref, kept_ref):
+    out_ref[0:PACKED] = jnp.sum(in_ref[...], axis=0)
+    out_ref[PACKED:] = jnp.zeros((COUNT, SUB, LANE), jnp.float32)
+    kept_ref[...] = jnp.zeros((COUNT, SUB, LANE), jnp.float32)
+
+
+def split_kernel(in_ref, out_ref, kept_ref):
+    out_ref[0:PACKED] = jnp.zeros((PACKED, SUB, LANE), jnp.float32)
+    out_ref[PACKED:] = in_ref[:, 0:SUB, :]
+    kept_ref[...] = in_ref[:, SUB:, :]
 
 
 def sum_kernel(in_ref, out_ref):
@@ -68,8 +84,8 @@
         out_ref[k] = total
 
 
-def mix_kernel(width_ref, dist_ref, slab_ref, out_ref):
-    packed = jnp.exp(-jnp.sum(dist_ref[...], axis=0) / width_ref[0:1])
+def mix_kernel(core_ref, width_ref, both_ref, kept_ref, slab_ref, out_ref):
+    packed = jnp.exp(-both_ref[0, 0:PACKED].reshape(PACK, LANE))
     both = jnp.concatenate([packed, pltpu.roll(packed, COUNT, 1)], axis=0)
     lane, row = iota((HALF, LANE), 1), iota((HALF, LANE), 0)
     top = jnp.where((lane > row) & (lane < COUNT), both, 0.0)
@@ -81,7 +97,8 @@
     pull = 2.0 / width_ref[0:1, 0:1]
     own = pull * rowsum
     x = jnp.concatenate([slab_ref[:, s, :] for s in range(SUB)], axis=1)
-    g = jnp.concatenate([slab_ref[:, SUB + s, :] for s in range(SUB)], axis=1)
+    grads = jnp.where(core_ref[...] == 0.0, both_ref[1, PACKED:], kept_ref[...])
+    g = jnp.concatenate([grads[:, s, :] for s in range(SUB)], axis=1)
     mixed = dot(kernel, g - pull * x, ((1,), (0,)))
     mixed = (mixed + own * x) * (1.0 / COUNT)
     for s in range(SUB):
@@ -149,26 +166,50 @@
     return lax.all_to_all(array, axes, split_axis=0, concat_axis=0, tiled=True)
 
 
+def share(array):
+    return lax.all_gather(array, "core", axis=0, tiled=False)
+
+
 def body(particles, gradients, first_moment, second_moment, spread):
     _, rows, cols = particles.shape
     entries = rows * cols * lax.axis_size("x") * lax.axis_size("core")
-    plane = lax.axis_size("y") * lax.axis_size("x") * lax.axis_size("core")
+    plane = lax.axis_size("y") * lax.axis_size("x")
     depth = lax.axis_size("z")
+    core = lax.axis_index("core")
+    width = jnp.full((SUB, LANE), spread * entries, jnp.float32)
+    which = jnp.full((1, SUB, LANE), core.astype(jnp.float32), jnp.float32)
+    payload = vmem(PACKED + COUNT, SUB, LANE)
     with jax.named_scope("gather_slab"):
-        both = call(
-            stack_kernel, vmem(COUNT, 2 * SUB, LANE), [ANYWHERE] * 2,
-            (tiles(particles[0]), tiles(gradients[0])),
-            scratch=[pltpu.SemaphoreType.DMA((2,))],
-        )
-        slab = exchange(both, RING)
+        slab = exchange(tiles(particles[0]), RING)
     with jax.named_scope("distances"):
-        part = call(dist_kernel, vmem(plane, PACK, LANE), [IN_VMEM], (slab,))
+        both = share(call(
+            pack_kernel, payload, [IN_VMEM, IN_VMEM, ANYWHERE], (width, slab, tiles(gradients[0])),
+            scratch=[pltpu.SemaphoreType.DMA],
+        ))
+
+    def reduce(both):
+        part = call(spread_kernel, vmem(plane, PACKED, SUB, LANE), [IN_VMEM], (both,))
         part = exchange(part, PLANE)
-        part = call(sum_kernel, vmem(depth, PACK, LANE), [IN_VMEM], (part,))
+        part = call(sum_kernel, vmem(depth, PACKED, SUB, LANE), [IN_VMEM], (part,))
         part = exchange(part, "z")
+        return call(
+            last_kernel, (payload, vmem(COUNT, SUB, LANE)), [IN_VMEM], (part,), out_specs=(IN_VMEM,) * 2
+        )
+
+    def gather(both):
+        grads = call(stack_kernel, vmem(COUNT, 2 * SUB, LANE), [IN_VMEM], (both,))
+        grads = exchange(grads, RING)
+        return call(
+            split_kernel, (payload, vmem(COUNT, SUB, LANE)), [IN_VMEM], (grads,), out_specs=(IN_VMEM,) * 2
+        )
+
+    with jax.named_scope("reduce_or_gather"):
+        mine, kept = lax.cond(core == 0, reduce, gather, both)
+        both = share(mine)
     with jax.named_scope("mix"):
-        width = jnp.full((SUB, LANE), spread * entries, jnp.float32)
-        mixed = call(mix_kernel, vmem(COUNT, SUB, LANE), [IN_VMEM] * 3, (width, part, slab))
+        mixed = call(
+            mix_kernel, vmem(COUNT, SUB, LANE), [IN_VMEM] * 5, (which, width, both, kept, slab)
+        )
     with jax.named_scope("return_slab"):
         direction = untiles(exchange(mixed, RING), rows, cols)
     with jax.named_scope("adam"):

time: 119 us -> 107 us (0.90)
  blocking collectives: 96 us -> 62.8 us
  starting transfers between devices: 3.51 us -> 19.3 us
  waiting for transfers between devices: 11.7 us -> 18.6 us
  Pallas kernels: 4.46 us -> 2.91 us
    all_to_all x3 -> x2, blocking collectives: 96 us -> 51.6 us  [exchange(): return lax.all_to_all(array, axes, split_axis=0, concat_axis=0, tiled=True)]
    all_to_all x1, starting transfers between devices: 3.51 us -> 19.3 us  [exchange(): return lax.all_to_all(array, axes, split_axis=0, concat_axis=0, tiled=True)]
    all_gather x0 -> x2, blocking collectives: none -> 11.2 us  [share(): return lax.all_gather(array, 'core', axis=0, tiled=False)]
    all_to_all x1, waiting for transfers between devices: 11.7 us -> 18.6 us  [exchange(): return lax.all_to_all(array, axes, split_axis=0, concat_axis=0, tiled=True)]
    pallas_call x5, Pallas kernels: 4.46 us -> 2.91 us  [call(): pl.pallas_call(kernel, out_shape=out_shape, in_specs=in_specs, out_specs=...]
where the time goes in v3:
time: 107 us; the launch traced here: 105 us
  blocking collectives  62.8 us (59%)
  starting transfers between devices  19.3 us (18%)
  waiting for transfers between devices  18.6 us (17%)
  Pallas kernels  2.91 us (3%)
  between operations  1.34 us (1%)
    all_to_all x2, blocking collectives, exchange(): return lax.all_to_all(array, axes, split_axis=0, concat_axis=0, tiled=True)  51.6 us
    all_to_all x1, starting transfers between devices, exchange(): return lax.all_to_all(array, axes, split_axis=0, concat_axis=0, tiled=True)  19.3 us
    all_to_all x1, waiting for transfers between devices, exchange(): return lax.all_to_all(array, axes, split_axis=0, concat_axis=0, tiled=True)  18.6 us
    all_gather x2, blocking collectives, share(): return lax.all_gather(array, 'core', axis=0, tiled=False)  11.2 us
    pallas_call x5, Pallas kernels, call(): pl.pallas_call(kernel, out_shape=out_shape, in_specs=in_specs, out_specs=...  2.91 us
  transfers between devices with their start and end apart: 1, of which 1 were waited for; matrix products, arithmetic and copies ran while one was open for 0% of the time, Pallas kernels for 0%

profile of v3, /device:TPU:1, one launch (start us, length us, event | category | flops | bytes accessed | tf_op | source)
XLA Modules:
  0.0 105.0 jit_solution(17249022709686878018)
XLA Ops:
  0.6 19.3 %all-to-all-start.3 = ((f32[64,8,128]{2,1,0:T(8,128)}), f32[64,8,128]{2,1,0:T(8,128)S(1)}, u32[]{:S(2)}, u32[]{:S(2)}) async-start(f32[64,8,128]{2,1,0:T(8,128)} %bitcast.27), calls=%async_computation.3 | async-start | bytes 524288 | tf_op jit(solution)/shard_map/gather_slab/all_to_all | solution.py:166
  20.6 18.6 %all-to-all-done.3.slab_ref = f32[64,8,128]{2,1,0:T(8,128)S(1)} async-done(((f32[64,8,128]{2,1,0:T(8,128)}), f32[64,8,128]{2,1,0:T(8,128)S(1)}, u32[]{:S(2)}, u32[]{:S(2)}) %all-to-all-start.3) | async-done | bytes 262176 | tf_op jit(solution)/shard_map/gather_slab/all_to_all | solution.py:166
  39.1 1.0 distances.1
  40.2 6.0 %all-gather = f32[132,8,128]{2,1,0:T(8,128)S(1)} all-gather(f32[66,8,128]{2,1,0:T(8,128)S(1)} %distances.1), channel_id=2, replica_groups=mesh['z'=16,'y'=4,'x'=4,'core'=2] {'core'}, dimensions={0}, use_global_device_ids=true | all-gather | bytes 811008 | tf_op jit(solution)/shard_map/distances/all_gather | solution.py:170
  46.2 26.4 %conditional.1 = ((f32[66,8,128]{2,1,0:T(8,128)S(1)}, f32[64,8,128]{2,1,0:T(8,128)S(1)})) conditional(s32[]{:T(128)} %convert_element_type.7, f32[2,66,8,128]{3,2,1,0:T(8,128)S(1)} %bitcast.24, f32[2,66,8,128]{3,2,1,0:T(8,128)S(1)} %bitcast.25), branch_computations={%region_0.0_spmd, %region_1.0_spmd} | conditional | bytes 1048584 | solution.py:207
  46.2 26.3 %all_to_all.22.in_ref = f32[64,16,128]{2,1,0:T(8,128)S(1)} all-to-all(f32[64,16,128]{2,1,0:T(8,128)S(1)} %branch_0_fun.2), channel_id=1, replica_groups=mesh['z'=16,'y'=4,'x'=4,'core'=2] {'z','y'}, dimensions={0} | all-to-all | bytes 1048576 | tf_op jit(solution)/shard_map/reduce_or_gather/cond/branch_0_fun/all_to_all | solution.py:166
  72.6 5.2 %all-gather.1 = f32[132,8,128]{2,1,0:T(8,128)S(1)} all-gather(f32[66,8,128]{2,1,0:T(8,128)S(1)} %get-tuple-element.12), channel_id=3, replica_groups=mesh['z'=16,'y'=4,'x'=4,'core'=2] {'core'}, dimensions={0}, use_global_device_ids=true | all-gather | bytes 811008 | tf_op jit(solution)/shard_map/reduce_or_gather/all_gather | solution.py:170
  77.8 0.0 copy-start.2
  77.8 0.7 mix.1
  78.6 0.0 copy-start
  78.6 0.0 copy-start.1
  78.6 25.3 %all_to_all.25 = f32[64,8,128]{2,1,0:T(8,128)S(1)} all-to-all(f32[64,8,128]{2,1,0:T(8,128)S(1)} %mix.1), channel_id=1, replica_groups=mesh['z'=16,'y'=4,'x'=4,'core'=2] {'z','y'}, dimensions={0} | all-to-all | bytes 524288 | tf_op jit(solution)/shard_map/return_slab/all_to_all | solution.py:166
  103.9 0.0 copy-done.2
  103.9 0.0 copy-done
  103.9 0.0 copy-done.1
  103.9 1.1 %adam.1 = (f32[32,2048]{1,0:T(8,128)}, f32[32,2048]{1,0:T(8,128)}, f32[32,2048]{1,0:T(8,128)}, f32[32,2048]{1,0:T(8,128)}) custom-call(f32[32,2048]{1,0:T(8,128)S(1)} %bitcast.28, f32[32,2048]{1,0:T(8,128)S(1)} %bitcast.30, f32[32,2048]{1,0:T(8,128)S(1)} %bitcast.31, f32[32,2048]{1,0:T(8,128)S(1)} %bitcast.29), custom_call_target="tpu_custom_call" | custom-call | tf_op jit(solution)/shard_map/adam/pallas_call | solution.py:139
  (4 shorter events, 0.1 us)
Async XLA Ops:
  0.6 38.5 %all-to-all-start.3 = ((f32[64,8,128]{2,1,0:T(8,128)}), f32[64,8,128]{2,1,0:T(8,128)S(1)}, u32[]{:S(2)}, u32[]{:S(2)}) async-start(f32[64,8,128]{2,1,0:T(8,128)} %bitcast.27), calls=%async_computation.3 | async-start | bytes 524288 | tf_op jit(solution)/shard_map/gather_slab/all_to_all | solution.py:166
  77.8 26.1 %copy-start.2 = (f32[1,32,2048]{2,1,0:T(8,128)S(1)}, f32[1,32,2048]{2,1,0:T(8,128)}, u32[]{:S(2)}) copy-start(f32[1,32,2048]{2,1,0:T(8,128)} %param.10) | copy-start | bytes 786436
  78.6 25.3 %copy-start = (f32[1,32,2048]{2,1,0:T(8,128)S(1)}, f32[1,32,2048]{2,1,0:T(8,128)}, u32[]{:S(2)}) copy-start(f32[1,32,2048]{2,1,0:T(8,128)} %param.7) | copy-start | bytes 786436
  78.6 25.3 %copy-start.1 = (f32[1,32,2048]{2,1,0:T(8,128)S(1)}, f32[1,32,2048]{2,1,0:T(8,128)}, u32[]{:S(2)}) copy-start(f32[1,32,2048]{2,1,0:T(8,128)} %param.9) | copy-start | bytes 786436

commit v4 on v3

--- a/solution.py
+++ b/solution.py
@@ -163,7 +163,13 @@
 
 
 def exchange(array, axes):
-    return lax.all_to_all(array, axes, split_axis=0, concat_axis=0, tiled=True)
+    places = [0]
+    for axis in axes:
+        size = lax.axis_size(axis)
+        places = [p * size + (i + size // 2) % size for p in places for i in range(size)]
+    return lax.all_to_all(
+        array, axes, split_axis=0, concat_axis=0, axis_index_groups=[places], tiled=True
+    )
 
 
 def share(array):
@@ -191,7 +197,7 @@
         part = call(spread_kernel, vmem(plane, PACKED, SUB, LANE), [IN_VMEM], (both,))
         part = exchange(part, PLANE)
         part = call(sum_kernel, vmem(depth, PACKED, SUB, LANE), [IN_VMEM], (part,))
-        part = exchange(part, "z")
+        part = exchange(part, ("z",))
         return call(
             last_kernel, (payload, vmem(COUNT, SUB, LANE)), [IN_VMEM], (part,), out_specs=(IN_VMEM,) * 2
         )

time: 107 us -> 100 us (0.935); the launches traced: 105 us -> 99.8 us
  waiting for transfers between devices: 18.6 us -> 10.3 us
  starting transfers between devices: 19.3 us -> 23.1 us
    all_to_all x1, waiting for transfers between devices: 18.6 us -> 10.3 us  [exchange(): lax.all_to_all(array, axes, split_axis=0, concat_axis=0, axis_index_group...]
    all_gather x2, blocking collectives: 11.2 us -> 6.63 us  [share(): return lax.all_gather(array, 'core', axis=0, tiled=False)]
    all_to_all x2, blocking collectives: 51.6 us -> 55.5 us  [exchange(): lax.all_to_all(array, axes, split_axis=0, concat_axis=0, axis_index_group...]
    all_to_all x1, starting transfers between devices: 19.3 us -> 23.1 us  [exchange(): lax.all_to_all(array, axes, split_axis=0, concat_axis=0, axis_index_group...]
where the time goes in v4:
time: 100 us; the launch traced here: 99.8 us
  blocking collectives  62.1 us (62%)
  starting transfers between devices  23.1 us (23%)
  waiting for transfers between devices  10.3 us (10%)
  Pallas kernels  2.91 us (3%)
  between operations  1.34 us (1%)
    all_to_all x2, blocking collectives, exchange(): lax.all_to_all(array, axes, split_axis=0, concat_axis=0, axis_index_group...  55.5 us
    all_to_all x1, starting transfers between devices, exchange(): lax.all_to_all(array, axes, split_axis=0, concat_axis=0, axis_index_group...  23.1 us
    all_to_all x1, waiting for transfers between devices, exchange(): lax.all_to_all(array, axes, split_axis=0, concat_axis=0, axis_index_group...  10.3 us
    all_gather x2, blocking collectives, share(): return lax.all_gather(array, 'core', axis=0, tiled=False)  6.63 us
    pallas_call x5, Pallas kernels, call(): pl.pallas_call(kernel, out_shape=out_shape, in_specs=in_specs, out_specs=...  2.91 us
  transfers between devices with their start and end apart: 1, of which 1 were waited for; matrix products, arithmetic and copies ran while one was open for 0% of the time, Pallas kernels for 0%

profile of v4, /device:TPU:1, one launch (start us, length us, event | category | flops | bytes accessed | tf_op | source)
XLA Modules:
  0.0 99.8 jit_solution(15685124323027504673)
XLA Ops:
  0.6 23.1 %all-to-all-start.3 = ((f32[64,8,128]{2,1,0:T(8,128)}), f32[64,8,128]{2,1,0:T(8,128)S(1)}, u32[]{:S(2)}, u32[]{:S(2)}) async-start(f32[64,8,128]{2,1,0:T(8,128)} %bitcast.27), calls=%async_computation.3 | async-start | bytes 524288 | tf_op jit(solution)/shard_map/gather_slab/all_to_all | solution.py:170
  24.4 10.3 %all-to-all-done.3.slab_ref = f32[64,8,128]{2,1,0:T(8,128)S(1)} async-done(((f32[64,8,128]{2,1,0:T(8,128)}), f32[64,8,128]{2,1,0:T(8,128)S(1)}, u32[]{:S(2)}, u32[]{:S(2)}) %all-to-all-start.3) | async-done | bytes 262176 | tf_op jit(solution)/shard_map/gather_slab/all_to_all | solution.py:170
  34.7 1.0 %distances.1 = f32[66,8,128]{2,1,0:T(8,128)S(1)} custom-call(f32[8,128]{1,0:T(8,128)S(1)} %broadcast_in_dim.19.width_ref, f32[64,8,128]{2,1,0:T(8,128)S(1)} %all-to-all-done.3.slab_ref, f32[64,8,128]{2,1,0:T(8,128)} %bitcast.32), custom_call_target="tpu_custom_call" | custom-call | tf_op jit(solution)/shard_map/distances/pallas_call | solution.py:139
  35.7 3.8 %all-gather = f32[132,8,128]{2,1,0:T(8,128)S(1)} all-gather(f32[66,8,128]{2,1,0:T(8,128)S(1)} %distances.1), channel_id=2, replica_groups=mesh['z'=16,'y'=4,'x'=4,'core'=2] {'core'}, dimensions={0}, use_global_device_ids=true | all-gather | bytes 811008 | tf_op jit(solution)/shard_map/distances/all_gather | solution.py:176
  39.6 29.9 %conditional.1 = ((f32[66,8,128]{2,1,0:T(8,128)S(1)}, f32[64,8,128]{2,1,0:T(8,128)S(1)})) conditional(s32[]{:T(128)} %convert_element_type.7, f32[2,66,8,128]{3,2,1,0:T(8,128)S(1)} %bitcast.24, f32[2,66,8,128]{3,2,1,0:T(8,128)S(1)} %bitcast.25), branch_computations={%region_0.0_spmd, %region_1.0_spmd} | conditional | bytes 1048584 | solution.py:213
  39.6 29.8 %all_to_all.22.in_ref = f32[64,16,128]{2,1,0:T(8,128)S(1)} all-to-all(f32[64,16,128]{2,1,0:T(8,128)S(1)} %branch_0_fun.2), channel_id=1, replica_groups={{272,280,256,264,304,312,288,296,336,344,320,328,368,376,352,360,400,40..., dimensions={0} | all-to-all | bytes 1048576 | tf_op jit(solution)/shard_map/reduce_or_gather/cond/branch_0_fun/all_to_all | solution.py:170
  69.4 2.8 %all-gather.1 = f32[132,8,128]{2,1,0:T(8,128)S(1)} all-gather(f32[66,8,128]{2,1,0:T(8,128)S(1)} %get-tuple-element.12), channel_id=3, replica_groups=mesh['z'=16,'y'=4,'x'=4,'core'=2] {'core'}, dimensions={0}, use_global_device_ids=true | all-gather | bytes 811008 | tf_op jit(solution)/shard_map/reduce_or_gather/all_gather | solution.py:176
  72.3 0.0 copy-start.2
  72.3 0.7 mix.1
  73.0 0.0 copy-start
  73.0 0.0 copy-start.1
  73.0 25.7 %all_to_all.25 = f32[64,8,128]{2,1,0:T(8,128)S(1)} all-to-all(f32[64,8,128]{2,1,0:T(8,128)S(1)} %mix.1), channel_id=1, replica_groups={{272,280,256,264,304,312,288,296,336,344,320,328,368,376,352,360,400,40..., dimensions={0} | all-to-all | bytes 524288 | tf_op jit(solution)/shard_map/return_slab/all_to_all | solution.py:170
  98.7 0.0 copy-done.2
  98.8 0.0 copy-done
  98.8 0.0 copy-done.1
  98.8 1.1 %adam.1 = (f32[32,2048]{1,0:T(8,128)}, f32[32,2048]{1,0:T(8,128)}, f32[32,2048]{1,0:T(8,128)}, f32[32,2048]{1,0:T(8,128)}) custom-call(f32[32,2048]{1,0:T(8,128)S(1)} %bitcast.28, f32[32,2048]{1,0:T(8,128)S(1)} %bitcast.30, f32[32,2048]{1,0:T(8,128)S(1)} %bitcast.31, f32[32,2048]{1,0:T(8,128)S(1)} %bitcast.29), custom_call_target="tpu_custom_call" | custom-call | tf_op jit(solution)/shard_map/adam/pallas_call | solution.py:139
  (4 shorter events, 0.1 us)
Async XLA Ops:
  0.6 34.1 %all-to-all-start.3 = ((f32[64,8,128]{2,1,0:T(8,128)}), f32[64,8,128]{2,1,0:T(8,128)S(1)}, u32[]{:S(2)}, u32[]{:S(2)}) async-start(f32[64,8,128]{2,1,0:T(8,128)} %bitcast.27), calls=%async_computation.3 | async-start | bytes 524288 | tf_op jit(solution)/shard_map/gather_slab/all_to_all | solution.py:170
  72.3 26.5 %copy-start.2 = (f32[1,32,2048]{2,1,0:T(8,128)S(1)}, f32[1,32,2048]{2,1,0:T(8,128)}, u32[]{:S(2)}) copy-start(f32[1,32,2048]{2,1,0:T(8,128)} %param.10) | copy-start | bytes 786436
  73.0 25.7 %copy-start = (f32[1,32,2048]{2,1,0:T(8,128)S(1)}, f32[1,32,2048]{2,1,0:T(8,128)}, u32[]{:S(2)}) copy-start(f32[1,32,2048]{2,1,0:T(8,128)} %param.7) | copy-start | bytes 786436
  73.0 25.7 %copy-start.1 = (f32[1,32,2048]{2,1,0:T(8,128)S(1)}, f32[1,32,2048]{2,1,0:T(8,128)}, u32[]{:S(2)}) copy-start(f32[1,32,2048]{2,1,0:T(8,128)} %param.9) | copy-start | bytes 786436

commit v5 on v4

--- a/solution.py
+++ b/solution.py
@@ -1,3 +1,5 @@
+import math
+
 import jax
 import jax.numpy as jnp
 from jax import lax
@@ -34,9 +36,7 @@
     return lax.broadcasted_iota(jnp.int32, shape, dim)
 
 
-def pack_kernel(width_ref, slab_ref, g_ref, out_ref, sem):
-    copy = pltpu.make_async_copy(g_ref, out_ref.at[pl.ds(PACKED, COUNT)], sem)
-    copy.start()
+def pack_kernel(width_ref, slab_ref, out_ref):
     x = jnp.concatenate([slab_ref[:, s, :] for s in range(SUB)], axis=1)
     gram = dot(x, jnp.concatenate([x, x], axis=0), ((1,), (1,)))
     lane = lax.rem(iota((COUNT, LANE), 1), COUNT)
@@ -52,18 +52,17 @@
     packed = jnp.where(iota((PACK, LANE), 1) < COUNT, both[:PACK], both[PACK:]) / width_ref[0:1]
     for k in range(PACKED):
         out_ref[k] = packed[k * SUB:(k + 1) * SUB]
-    copy.wait()
 
 
 def spread_kernel(both_ref, out_ref):
-    total = both_ref[0, 0:PACKED] + both_ref[1, 0:PACKED]
+    total = both_ref[0] + both_ref[1]
     for k in range(out_ref.shape[0]):
         out_ref[k] = total
 
 
 def stack_kernel(both_ref, out_ref):
-    out_ref[:, 0:SUB, :] = both_ref[0, PACKED:]
-    out_ref[:, SUB:, :] = both_ref[1, PACKED:]
+    out_ref[:, 0:SUB, :] = both_ref[0]
+    out_ref[:, SUB:, :] = both_ref[1]
 
 
 def last_kernel(in_ref, out_ref, kept_ref):
@@ -164,9 +163,10 @@
 
 def exchange(array, axes):
     places = [0]
-    for axis in axes:
+    for axis in sorted(axes, key="yxz".index):
         size = lax.axis_size(axis)
-        places = [p * size + (i + size // 2) % size for p in places for i in range(size)]
+        step = math.prod(lax.axis_size(a) for a in axes[axes.index(axis) + 1:])
+        places = [p + (i + size // 2) % size * step for p in places for i in range(size)]
     return lax.all_to_all(
         array, axes, split_axis=0, concat_axis=0, axis_index_groups=[places], tiled=True
     )
@@ -186,14 +186,12 @@
     which = jnp.full((1, SUB, LANE), core.astype(jnp.float32), jnp.float32)
     payload = vmem(PACKED + COUNT, SUB, LANE)
     with jax.named_scope("gather_slab"):
+        grads = share(tiles(gradients[0]))
         slab = exchange(tiles(particles[0]), RING)
     with jax.named_scope("distances"):
-        both = share(call(
-            pack_kernel, payload, [IN_VMEM, IN_VMEM, ANYWHERE], (width, slab, tiles(gradients[0])),
-            scratch=[pltpu.SemaphoreType.DMA],
-        ))
-
-    def reduce(both):
+        both = share(call(pack_kernel, vmem(PACKED, SUB, LANE), [IN_VMEM] * 2, (width, slab)))
+
+    def reduce(both, grads):
         part = call(spread_kernel, vmem(plane, PACKED, SUB, LANE), [IN_VMEM], (both,))
         part = exchange(part, PLANE)
         part = call(sum_kernel, vmem(depth, PACKED, SUB, LANE), [IN_VMEM], (part,))
@@ -202,15 +200,15 @@
             last_kernel, (payload, vmem(COUNT, SUB, LANE)), [IN_VMEM], (part,), out_specs=(IN_VMEM,) * 2
         )
 
-    def gather(both):
-        grads = call(stack_kernel, vmem(COUNT, 2 * SUB, LANE), [IN_VMEM], (both,))
-        grads = exchange(grads, RING)
+    def gather(both, grads):
+        part = call(stack_kernel, vmem(COUNT, 2 * SUB, LANE), [IN_VMEM], (grads,))
+        part = exchange(part, RING)
         return call(
-            split_kernel, (payload, vmem(COUNT, SUB, LANE)), [IN_VMEM], (grads,), out_specs=(IN_VMEM,) * 2
+            split_kernel, (payload, vmem(COUNT, SUB, LANE)), [IN_VMEM], (part,), out_specs=(IN_VMEM,) * 2
         )
 
     with jax.named_scope("reduce_or_gather"):
-        mine, kept = lax.cond(core == 0, reduce, gather, both)
+        mine, kept = lax.cond(core == 0, reduce, gather, both, grads)
         both = share(mine)
     with jax.named_scope("mix"):
         mixed = call(

time: 100 us -> 100 us (level)
  waiting for transfers between devices: 10.3 us -> 7.86 us
  blocking collectives: 62.1 us -> 64.5 us
    all_to_all x1, waiting for transfers between devices: 10.3 us -> 7.86 us  [exchange(): lax.all_to_all(array, axes, split_axis=0, concat_axis=0, axis_index_group...]
    all_gather x2 -> x3, blocking collectives: 6.63 us -> 8.94 us  [share(): return lax.all_gather(array, 'core', axis=0, tiled=False)]
where the time goes in v5:
time: 100 us; the launch traced here: 99.8 us
  blocking collectives  64.5 us (64%)
  starting transfers between devices  23.3 us (23%)
  waiting for transfers between devices  7.86 us (8%)
  Pallas kernels  2.74 us (3%)
  between operations  1.35 us (1%)
    all_to_all x2, blocking collectives, exchange(): lax.all_to_all(array, axes, split_axis=0, concat_axis=0, axis_index_group...  55.5 us
    all_to_all x1, starting transfers between devices, exchange(): lax.all_to_all(array, axes, split_axis=0, concat_axis=0, axis_index_group...  23.3 us
    all_gather x3, blocking collectives, share(): return lax.all_gather(array, 'core', axis=0, tiled=False)  8.94 us
    all_to_all x1, waiting for transfers between devices, exchange(): lax.all_to_all(array, axes, split_axis=0, concat_axis=0, axis_index_group...  7.86 us
    pallas_call x5, Pallas kernels, call(): pl.pallas_call(kernel, out_shape=out_shape, in_specs=in_specs, out_specs=...  2.74 us
  transfers between devices with their start and end apart: 1, of which 1 were waited for; matrix products, arithmetic and copies ran while one was open for 0% of the time, Pallas kernels for 0%

profile of v5, /device:TPU:1, one launch (start us, length us, event | category | flops | bytes accessed | tf_op | source)
XLA Modules:
  0.0 99.8 jit_solution(906883602866983844)
XLA Ops:
  0.6 0.0 copy-start.3
  0.6 23.3 %all-to-all-start.3 = ((f32[64,8,128]{2,1,0:T(8,128)}), f32[64,8,128]{2,1,0:T(8,128)S(1)}, u32[]{:S(2)}, u32[]{:S(2)}) async-start(f32[64,8,128]{2,1,0:T(8,128)} %bitcast.25), calls=%async_computation.3 | async-start | bytes 524288 | tf_op jit(solution)/shard_map/gather_slab/all_to_all | solution.py:170
  24.6 0.0 copy-done.3
  24.6 3.0 %all_gather.21 = f32[2,64,8,128]{3,2,1,0:T(8,128)S(1)} all-gather(f32[1,64,8,128]{3,2,1,0:T(8,128)S(1)} %bitcast.31), channel_id=1, replica_groups=mesh['z'=16,'y'=4,'x'=4,'core'=2] {'core'}, dimensions={0}, use_global_device_ids=true | all-gather | bytes 786432 | tf_op jit(solution)/shard_map/gather_slab/all_gather | solution.py:176
  27.7 7.9 %all-to-all-done.3.slab_ref = f32[64,8,128]{2,1,0:T(8,128)S(1)} async-done(((f32[64,8,128]{2,1,0:T(8,128)}), f32[64,8,128]{2,1,0:T(8,128)S(1)}, u32[]{:S(2)}, u32[]{:S(2)}) %all-to-all-start.3) | async-done | bytes 262176 | tf_op jit(solution)/shard_map/gather_slab/all_to_all | solution.py:170
  35.5 0.9 distances.1
  36.4 2.7 %all-gather = f32[4,8,128]{2,1,0:T(8,128)S(1)} all-gather(f32[2,8,128]{2,1,0:T(8,128)S(1)} %distances.1), channel_id=2, replica_groups=mesh['z'=16,'y'=4,'x'=4,'core'=2] {'core'}, dimensions={0}, use_global_device_ids=true | all-gather | bytes 24576 | tf_op jit(solution)/shard_map/distances/all_gather | solution.py:176
  39.1 29.5 %conditional.1 = ((f32[66,8,128]{2,1,0:T(8,128)S(1)}, f32[64,8,128]{2,1,0:T(8,128)S(1)})) conditional(s32[]{:T(128)} %convert_element_type.7, f32[2,64,8,128]{3,2,1,0:T(8,128)S(1)} %all_gather.21, (f32[4,8,128]{2,1,0:T(8,128)S(1)}) %tuple.15), branch_computations={%region_0.0_spmd, %region_1.0_spmd} | conditional | bytes 1048584 | solution.py:211
  39.2 29.4 %all_to_all.22.in_ref = f32[64,16,128]{2,1,0:T(8,128)S(1)} all-to-all(f32[64,16,128]{2,1,0:T(8,128)S(1)} %branch_0_fun.2), channel_id=1, replica_groups={{272,304,336,368,400,432,464,496,16,48,80,112,144,176,208,240,280,312,3..., dimensions={0} | all-to-all | bytes 1048576 | tf_op jit(solution)/shard_map/reduce_or_gather/cond/branch_0_fun/all_to_all | solution.py:170
  68.6 3.2 %all-gather.1 = f32[132,8,128]{2,1,0:T(8,128)S(1)} all-gather(f32[66,8,128]{2,1,0:T(8,128)S(1)} %get-tuple-element.12), channel_id=3, replica_groups=mesh['z'=16,'y'=4,'x'=4,'core'=2] {'core'}, dimensions={0}, use_global_device_ids=true | all-gather | bytes 811008 | tf_op jit(solution)/shard_map/reduce_or_gather/all_gather | solution.py:176
  71.8 0.0 copy-start.2
  71.8 0.7 mix.1
  72.5 0.0 copy-start
  72.5 0.0 copy-start.1
  72.5 26.1 %all_to_all.25 = f32[64,8,128]{2,1,0:T(8,128)S(1)} all-to-all(f32[64,8,128]{2,1,0:T(8,128)S(1)} %mix.1), channel_id=1, replica_groups={{272,304,336,368,400,432,464,496,16,48,80,112,144,176,208,240,280,312,3..., dimensions={0} | all-to-all | bytes 524288 | tf_op jit(solution)/shard_map/return_slab/all_to_all | solution.py:170
  98.7 0.0 copy-done.2
  98.7 0.0 copy-done
  98.7 0.0 copy-done.1
  98.7 1.1 %adam.1 = (f32[32,2048]{1,0:T(8,128)}, f32[32,2048]{1,0:T(8,128)}, f32[32,2048]{1,0:T(8,128)}, f32[32,2048]{1,0:T(8,128)}) custom-call(f32[32,2048]{1,0:T(8,128)S(1)} %bitcast.26, f32[32,2048]{1,0:T(8,128)S(1)} %bitcast.28, f32[32,2048]{1,0:T(8,128)S(1)} %bitcast.29, f32[32,2048]{1,0:T(8,128)S(1)} %bitcast.27), custom_call_target="tpu_custom_call" | custom-call | tf_op jit(solution)/shard_map/adam/pallas_call | solution.py:138
  (4 shorter events, 0.1 us)
Async XLA Ops:
  0.6 24.0 %copy-start.3 = (f32[1,32,2048]{2,1,0:T(8,128)S(1)}, f32[1,32,2048]{2,1,0:T(8,128)}, u32[]{:S(2)}) copy-start(f32[1,32,2048]{2,1,0:T(8,128)} %param.8) | copy-start | bytes 786436
  0.6 34.9 %all-to-all-start.3 = ((f32[64,8,128]{2,1,0:T(8,128)}), f32[64,8,128]{2,1,0:T(8,128)S(1)}, u32[]{:S(2)}, u32[]{:S(2)}) async-start(f32[64,8,128]{2,1,0:T(8,128)} %bitcast.25), calls=%async_computation.3 | async-start | bytes 524288 | tf_op jit(solution)/shard_map/gather_slab/all_to_all | solution.py:170
  71.8 26.9 %copy-start.2 = (f32[1,32,2048]{2,1,0:T(8,128)S(1)}, f32[1,32,2048]{2,1,0:T(8,128)}, u32[]{:S(2)}) copy-start(f32[1,32,2048]{2,1,0:T(8,128)} %param.10) | copy-start | bytes 786436
  72.5 26.2 %copy-start = (f32[1,32,2048]{2,1,0:T(8,128)S(1)}, f32[1,32,2048]{2,1,0:T(8,128)}, u32[]{:S(2)}) copy-start(f32[1,32,2048]{2,1,0:T(8,128)} %param.7) | copy-start | bytes 786436
  72.5 26.2 %copy-start.1 = (f32[1,32,2048]{2,1,0:T(8,128)S(1)}, f32[1,32,2048]{2,1,0:T(8,128)}, u32[]{:S(2)}) copy-start(f32[1,32,2048]{2,1,0:T(8,128)} %param.9) | copy-start | bytes 786436

commit v6 on v5

--- a/solution.py
+++ b/solution.py
@@ -32,13 +32,32 @@
     )
 
 
+def thirds(a):
+    high = a.astype(jnp.bfloat16)
+    rest = a - high.astype(jnp.float32)
+    mid = rest.astype(jnp.bfloat16)
+    return high, mid, (rest - mid.astype(jnp.float32)).astype(jnp.bfloat16)
+
+
+def product(a, b, dims):
+    return lax.dot_general(a, b, (dims, ((), ())), preferred_element_type=jnp.float32)
+
+
 def iota(shape, dim):
     return lax.broadcasted_iota(jnp.int32, shape, dim)
 
 
-def pack_kernel(width_ref, slab_ref, out_ref):
-    x = jnp.concatenate([slab_ref[:, s, :] for s in range(SUB)], axis=1)
-    gram = dot(x, jnp.concatenate([x, x], axis=0), ((1,), (1,)))
+def pack_kernel(slab_ref, out_ref):
+    x = jnp.concatenate([slab_ref[:, s, :] for s in range(2 * SUB)], axis=1)
+    high, mid, low = thirds(x)
+    parts = product(
+        jnp.concatenate([high, mid, low], axis=0),
+        jnp.concatenate([high, high, mid, mid, low, low], axis=0),
+        ((1,), (1,)),
+    )
+    block = lambda i, j: parts[i * COUNT:(i + 1) * COUNT, j * LANE:(j + 1) * LANE]
+    gram = block(1, 1) + (block(0, 2) + block(2, 0))
+    gram = block(0, 0) + ((block(0, 1) + block(1, 0)) + gram)
     lane = lax.rem(iota((COUNT, LANE), 1), COUNT)
     on_diag = jnp.where(lane == iota((COUNT, LANE), 0), gram, 0.0)
     norm_row = jnp.sum(on_diag, axis=0, keepdims=True)
@@ -49,32 +68,55 @@
     lane = lax.rem(iota((HALF, LANE), 1), COUNT)
     keep = lane > iota((HALF, LANE), 0)
     both = jnp.where(keep, top, low)
-    packed = jnp.where(iota((PACK, LANE), 1) < COUNT, both[:PACK], both[PACK:]) / width_ref[0:1]
-    for k in range(PACKED):
-        out_ref[k] = packed[k * SUB:(k + 1) * SUB]
-
-
-def spread_kernel(both_ref, out_ref):
-    total = both_ref[0] + both_ref[1]
-    for k in range(out_ref.shape[0]):
-        out_ref[k] = total
-
-
-def stack_kernel(both_ref, out_ref):
-    out_ref[:, 0:SUB, :] = both_ref[0]
-    out_ref[:, SUB:, :] = both_ref[1]
-
-
-def last_kernel(in_ref, out_ref, kept_ref):
+    packed = jnp.where(iota((PACK, LANE), 1) < COUNT, both[:PACK], both[PACK:])
+    for i in range(out_ref.shape[0]):
+        for k in range(PACKED):
+            out_ref[i, k] = packed[k * SUB:(k + 1) * SUB]
+
+
+def stack_kernel(first_ref, second_ref, out_ref):
+    out_ref[:, 0:SUB, :] = first_ref[...]
+    out_ref[:, SUB:, :] = second_ref[...]
+
+
+def last_kernel(in_ref, slab_ref, out_ref, kept_ref):
     out_ref[0:PACKED] = jnp.sum(in_ref[...], axis=0)
-    out_ref[PACKED:] = jnp.zeros((COUNT, SUB, LANE), jnp.float32)
-    kept_ref[...] = jnp.zeros((COUNT, SUB, LANE), jnp.float32)
-
-
-def split_kernel(in_ref, out_ref, kept_ref):
-    out_ref[0:PACKED] = jnp.zeros((PACKED, SUB, LANE), jnp.float32)
-    out_ref[PACKED:] = in_ref[:, 0:SUB, :]
-    kept_ref[...] = in_ref[:, SUB:, :]
+    out_ref[PACKED:] = slab_ref[:, 0:SUB, :]
+    kept_ref[...] = slab_ref[:, SUB:, :]
+
+
+def turn_kernel(first_ref, second_ref, out_ref):
+    depth = COUNT // 4
+    for y in range(4):
+        for z in range(depth):
+            out_ref[z * 4 + y, 0:SUB, :] = first_ref[y * depth + z]
+            out_ref[z * 4 + y, SUB:, :] = second_ref[y * depth + z]
+
+
+def split_kernel(width_ref, slab_ref, out_ref, kept_ref):
+    out_ref[0:PACKED] = jnp.broadcast_to(width_ref[...][None], (PACKED, SUB, LANE))
+    depth = COUNT // 4
+    for y in range(4):
+        for z in range(depth):
+            out_ref[PACKED + y * depth + z] = slab_ref[z * 4 + y, SUB:, :]
+            kept_ref[y * depth + z] = slab_ref[z * 4 + y, 0:SUB, :]
+
+
+def choose_kernel(x_ref, g_ref, send_ref, own_ref, sems):
+    core = lax.axis_index("core")
+
+    def fetch(send, own):
+        copies = [
+            pltpu.make_async_copy(send, send_ref, sems.at[0]),
+            pltpu.make_async_copy(own, own_ref, sems.at[1]),
+        ]
+        for copy in copies:
+            copy.start()
+        for copy in copies:
+            copy.wait()
+
+    pl.when(core == 0)(lambda: fetch(x_ref, g_ref))
+    pl.when(core != 0)(lambda: fetch(g_ref, x_ref))
 
 
 def sum_kernel(in_ref, out_ref):
@@ -83,8 +125,9 @@
         out_ref[k] = total
 
 
-def mix_kernel(core_ref, width_ref, both_ref, kept_ref, slab_ref, out_ref):
-    packed = jnp.exp(-both_ref[0, 0:PACKED].reshape(PACK, LANE))
+def mix_kernel(core_ref, both_ref, kept_ref, out_ref):
+    width = both_ref[0, 0][0:1]
+    packed = jnp.exp(-both_ref[1, 0:PACKED].reshape(PACK, LANE) / width)
     both = jnp.concatenate([packed, pltpu.roll(packed, COUNT, 1)], axis=0)
     lane, row = iota((HALF, LANE), 1), iota((HALF, LANE), 0)
     top = jnp.where((lane > row) & (lane < COUNT), both, 0.0)
@@ -93,10 +136,12 @@
     eye = jnp.where(iota((LANE, LANE), 0) == iota((LANE, LANE), 1), 1.0, 0.0)
     kernel = (half + half.T + eye)[:COUNT, :COUNT]
     rowsum = jnp.sum(kernel, axis=1, keepdims=True)
-    pull = 2.0 / width_ref[0:1, 0:1]
+    pull = 2.0 / width[:, 0:1]
     own = pull * rowsum
-    x = jnp.concatenate([slab_ref[:, s, :] for s in range(SUB)], axis=1)
-    grads = jnp.where(core_ref[...] == 0.0, both_ref[1, PACKED:], kept_ref[...])
+    second = core_ref[...] == 1.0
+    parts = jnp.where(second, kept_ref[...], both_ref[1, PACKED:])
+    grads = jnp.where(second, both_ref[0, PACKED:], kept_ref[...])
+    x = jnp.concatenate([parts[:, s, :] for s in range(SUB)], axis=1)
     g = jnp.concatenate([grads[:, s, :] for s in range(SUB)], axis=1)
     mixed = dot(kernel, g - pull * x, ((1,), (0,)))
     mixed = (mixed + own * x) * (1.0 / COUNT)
@@ -182,37 +227,44 @@
     plane = lax.axis_size("y") * lax.axis_size("x")
     depth = lax.axis_size("z")
     core = lax.axis_index("core")
-    width = jnp.full((SUB, LANE), spread * entries, jnp.float32)
     which = jnp.full((1, SUB, LANE), core.astype(jnp.float32), jnp.float32)
     payload = vmem(PACKED + COUNT, SUB, LANE)
-    with jax.named_scope("gather_slab"):
-        grads = share(tiles(gradients[0]))
-        slab = exchange(tiles(particles[0]), RING)
-    with jax.named_scope("distances"):
-        both = share(call(pack_kernel, vmem(PACKED, SUB, LANE), [IN_VMEM] * 2, (width, slab)))
-
-    def reduce(both, grads):
-        part = call(spread_kernel, vmem(plane, PACKED, SUB, LANE), [IN_VMEM], (both,))
+    with jax.named_scope("swap"):
+        x, g = tiles(particles[0]), tiles(gradients[0])
+        send, own = call(
+            choose_kernel, (vmem(COUNT, SUB, LANE),) * 2, [ANYWHERE] * 2, (x, g), out_specs=(IN_VMEM,) * 2,
+            scratch=[pltpu.SemaphoreType.DMA((2,))],
+        )
+        others = share(send)
+
+    def reduce(own, others, spread):
+        slab = call(stack_kernel, vmem(COUNT, 2 * SUB, LANE), [IN_VMEM] * 2, (others[0], own))
+        slab = exchange(slab, RING)
+        part = call(pack_kernel, vmem(plane, PACKED, SUB, LANE), [IN_VMEM], (slab,))
         part = exchange(part, PLANE)
         part = call(sum_kernel, vmem(depth, PACKED, SUB, LANE), [IN_VMEM], (part,))
         part = exchange(part, ("z",))
         return call(
-            last_kernel, (payload, vmem(COUNT, SUB, LANE)), [IN_VMEM], (part,), out_specs=(IN_VMEM,) * 2
-        )
-
-    def gather(both, grads):
-        part = call(stack_kernel, vmem(COUNT, 2 * SUB, LANE), [IN_VMEM], (grads,))
-        part = exchange(part, RING)
+            last_kernel, (payload, vmem(COUNT, SUB, LANE)), [IN_VMEM] * 2, (part, slab), out_specs=(IN_VMEM,) * 2
+        )
+
+    def gather(own, others, spread):
+        first = exchange(own, ("y",))
+        second = exchange(others[1], ("y",))
+        slab = call(turn_kernel, vmem(COUNT, 2 * SUB, LANE), [IN_VMEM] * 2, (first, second))
+        slab = exchange(slab, ("z",))
+        width = jnp.full((SUB, LANE), spread * entries, jnp.float32)
         return call(
-            split_kernel, (payload, vmem(COUNT, SUB, LANE)), [IN_VMEM], (part,), out_specs=(IN_VMEM,) * 2
+            split_kernel, (payload, vmem(COUNT, SUB, LANE)), [IN_VMEM] * 2, (width, slab),
+            out_specs=(IN_VMEM,) * 2
         )
 
     with jax.named_scope("reduce_or_gather"):
-        mine, kept = lax.cond(core == 0, reduce, gather, both, grads)
+        mine, kept = lax.cond(core == 1, reduce, gather, own, others, spread)
         both = share(mine)
     with jax.named_scope("mix"):
         mixed = call(
-            mix_kernel, vmem(COUNT, SUB, LANE), [IN_VMEM] * 5, (which, width, both, kept, slab)
+            mix_kernel, vmem(COUNT, SUB, LANE), [IN_VMEM] * 3, (which, both, kept)
         )
     with jax.named_scope("return_slab"):
         direction = untiles(exchange(mixed, RING), rows, cols)

time: 100 us -> 97.1 us (0.971)
  blocking collectives: 64.5 us -> 92.2 us
  starting transfers between devices: 23.3 us -> 0 us
  waiting for transfers between devices: 7.86 us -> 0 us
  Pallas kernels: 2.74 us -> 3.85 us
    all_to_all x2 -> x4, blocking collectives: 55.5 us -> 81.3 us  [exchange(): lax.all_to_all(array, axes, split_axis=0, concat_axis=0, axis_index_group...]
    all_to_all x1 -> x0, starting transfers between devices: 23.3 us -> none  [exchange(): lax.all_to_all(array, axes, split_axis=0, concat_axis=0, axis_index_group...]
    all_to_all x1 -> x0, waiting for transfers between devices: 7.86 us -> none  [exchange(): lax.all_to_all(array, axes, split_axis=0, concat_axis=0, axis_index_group...]
    all_gather x3 -> x2, blocking collectives: 8.94 us -> 10.9 us  [share(): return lax.all_gather(array, 'core', axis=0, tiled=False)]
    pallas_call x5 -> x7, Pallas kernels: 2.74 us -> 3.85 us  [call(): pl.pallas_call(kernel, out_shape=out_shape, in_specs=in_specs, out_specs=...]
  transfers between devices with their start and end apart: 1 -> 0, of which waited for: 1 -> 0; matrix products, arithmetic and copies ran while one was open for 0% -> 0% of each run, Pallas kernels for 0% -> 0%
where the time goes in v6:
time: 97.1 us; the launch traced here: 96.8 us
  blocking collectives  92.2 us (95%)
  Pallas kernels  3.85 us (4%)
    all_to_all x4, blocking collectives, exchange(): lax.all_to_all(array, axes, split_axis=0, concat_axis=0, axis_index_group...  81.3 us
    all_gather x2, blocking collectives, share(): return lax.all_gather(array, 'core', axis=0, tiled=False)  10.9 us
    pallas_call x7, Pallas kernels, call(): pl.pallas_call(kernel, out_shape=out_shape, in_specs=in_specs, out_specs=...  3.85 us

profile of v6, /device:TPU:1, one launch (start us, length us, event | category | flops | bytes accessed | tf_op | source)
XLA Modules:
  0.0 96.8 jit_solution(13328108150555646773)
XLA Ops:
  0.6 1.1 %swap.1 = (f32[64,8,128]{2,1,0:T(8,128)S(1)}, f32[64,8,128]{2,1,0:T(8,128)S(1)}) custom-call(f32[64,8,128]{2,1,0:T(8,128)} %bitcast.29, f32[64,8,128]{2,1,0:T(8,128)} %bitcast.36), custom_call_target="tpu_custom_call" | custom-call | tf_op jit(solution)/shard_map/swap/pallas_call | solution.py:183
  1.7 8.7 %all-gather = f32[128,8,128]{2,1,0:T(8,128)S(1)} all-gather(f32[64,8,128]{2,1,0:T(8,128)S(1)} %get-tuple-element.28), channel_id=2, replica_groups=mesh['z'=16,'y'=4,'x'=4,'core'=2] {'core'}, dimensions={0}, use_global_device_ids=true | all-gather | bytes 786432 | tf_op jit(solution)/shard_map/swap/all_gather | solution.py:221
  10.4 55.5 %conditional.1 = ((f32[66,8,128]{2,1,0:T(8,128)S(1)}, f32[64,8,128]{2,1,0:T(8,128)S(1)})) conditional(s32[]{:T(128)} %convert_element_type.7, (f32[]{:T(128)}, f32[64,8,128]{2,1,0:T(8,128)S(1)}, f32[2,64,8,128]{3,2,1,0:T(8,128)S(1)}) %tuple.21, (f32[2,64,8,128]{3,2,1,0:T(8,128)S(1)}, f32[64,8,128]{2,1,0:T(8,128)S(1)}) %tuple.22), branch_computations={%region_0.0_spmd, %region_1.0_spmd} | conditional | flops 1 | bytes 3149880 | solution.py:263
  10.4 28.8 %all_to_all.31.slab_ref = f32[64,16,128]{2,1,0:T(8,128)S(1)} all-to-all(f32[64,16,128]{2,1,0:T(8,128)S(1)} %branch_1_fun.4), channel_id=1, replica_groups={{272,304,336,368,400,432,464,496,16,48,80,112,144,176,208,240,280,312,3..., dimensions={0} | all-to-all | bytes 1048576 | tf_op jit(solution)/shard_map/reduce_or_gather/cond/branch_1_fun/all_to_all | solution.py:215
  39.3 0.9 branch_1_fun.5
  40.2 10.1 %all_to_all.32.in_ref = f32[16,2,8,128]{3,2,1,0:T(8,128)S(1)} all-to-all(f32[16,2,8,128]{3,2,1,0:T(8,128)S(1)} %branch_1_fun.5), channel_id=1, replica_groups={{20,22,16,18,28,30,24,26,4,6,0,2,12,14,8,10},{21,23,17,19,29,31,25,27,5..., dimensions={0} | all-to-all | bytes 262144 | tf_op jit(solution)/shard_map/reduce_or_gather/cond/branch_1_fun/all_to_all | solution.py:215
  50.3 15.5 %all_to_all.33.in_ref = f32[16,2,8,128]{3,2,1,0:T(8,128)S(1)} all-to-all(f32[16,2,8,128]{3,2,1,0:T(8,128)S(1)} %branch_1_fun.6), channel_id=1, replica_groups={{256,288,320,352,384,416,448,480,0,32,64,96,128,160,192,224},{257,289,3..., dimensions={0} | all-to-all | bytes 262144 | tf_op jit(solution)/shard_map/reduce_or_gather/cond/branch_1_fun/all_to_all | solution.py:215
  65.9 2.2 %all-gather.1 = f32[132,8,128]{2,1,0:T(8,128)S(1)} all-gather(f32[66,8,128]{2,1,0:T(8,128)S(1)} %get-tuple-element.29), channel_id=3, replica_groups=mesh['z'=16,'y'=4,'x'=4,'core'=2] {'core'}, dimensions={0}, use_global_device_ids=true | all-gather | bytes 811008 | tf_op jit(solution)/shard_map/reduce_or_gather/all_gather | solution.py:221
  68.1 0.0 copy-start.2
  68.1 0.7 mix.1
  68.8 0.0 copy-start
  68.8 0.0 copy-start.1
  68.8 26.9 %all_to_all.34 = f32[64,8,128]{2,1,0:T(8,128)S(1)} all-to-all(f32[64,8,128]{2,1,0:T(8,128)S(1)} %mix.1), channel_id=1, replica_groups={{272,304,336,368,400,432,464,496,16,48,80,112,144,176,208,240,280,312,3..., dimensions={0} | all-to-all | bytes 524288 | tf_op jit(solution)/shard_map/return_slab/all_to_all | solution.py:215
  95.7 0.0 copy-done.2
  95.7 0.0 copy-done
  95.7 0.0 copy-done.1
  95.7 1.1 %adam.1 = (f32[32,2048]{1,0:T(8,128)}, f32[32,2048]{1,0:T(8,128)}, f32[32,2048]{1,0:T(8,128)}, f32[32,2048]{1,0:T(8,128)}) custom-call(f32[32,2048]{1,0:T(8,128)S(1)} %bitcast.30, f32[32,2048]{1,0:T(8,128)S(1)} %bitcast.32, f32[32,2048]{1,0:T(8,128)S(1)} %bitcast.33, f32[32,2048]{1,0:T(8,128)S(1)} %bitcast.31), custom_call_target="tpu_custom_call" | custom-call | tf_op jit(solution)/shard_map/adam/pallas_call | solution.py:183
  (5 shorter events, 0.1 us)
Async XLA Ops:
  68.1 27.6 %copy-start.2 = (f32[1,32,2048]{2,1,0:T(8,128)S(1)}, f32[1,32,2048]{2,1,0:T(8,128)}, u32[]{:S(2)}) copy-start(f32[1,32,2048]{2,1,0:T(8,128)} %param.10) | copy-start | bytes 786436
  68.8 26.9 %copy-start = (f32[1,32,2048]{2,1,0:T(8,128)S(1)}, f32[1,32,2048]{2,1,0:T(8,128)}, u32[]{:S(2)}) copy-start(f32[1,32,2048]{2,1,0:T(8,128)} %param.7) | copy-start | bytes 786436
  68.8 26.9 %copy-start.1 = (f32[1,32,2048]{2,1,0:T(8,128)S(1)}, f32[1,32,2048]{2,1,0:T(8,128)}, u32[]{:S(2)}) copy-start(f32[1,32,2048]{2,1,0:T(8,128)} %param.9) | copy-start | bytes 786436

commit v7 on v6

--- a/solution.py
+++ b/solution.py
@@ -32,32 +32,13 @@
     )
 
 
-def thirds(a):
-    high = a.astype(jnp.bfloat16)
-    rest = a - high.astype(jnp.float32)
-    mid = rest.astype(jnp.bfloat16)
-    return high, mid, (rest - mid.astype(jnp.float32)).astype(jnp.bfloat16)
-
-
-def product(a, b, dims):
-    return lax.dot_general(a, b, (dims, ((), ())), preferred_element_type=jnp.float32)
-
-
 def iota(shape, dim):
     return lax.broadcasted_iota(jnp.int32, shape, dim)
 
 
 def pack_kernel(slab_ref, out_ref):
     x = jnp.concatenate([slab_ref[:, s, :] for s in range(2 * SUB)], axis=1)
-    high, mid, low = thirds(x)
-    parts = product(
-        jnp.concatenate([high, mid, low], axis=0),
-        jnp.concatenate([high, high, mid, mid, low, low], axis=0),
-        ((1,), (1,)),
-    )
-    block = lambda i, j: parts[i * COUNT:(i + 1) * COUNT, j * LANE:(j + 1) * LANE]
-    gram = block(1, 1) + (block(0, 2) + block(2, 0))
-    gram = block(0, 0) + ((block(0, 1) + block(1, 0)) + gram)
+    gram = dot(x, jnp.concatenate([x, x], axis=0), ((1,), (1,)))
     lane = lax.rem(iota((COUNT, LANE), 1), COUNT)
     on_diag = jnp.where(lane == iota((COUNT, LANE), 0), gram, 0.0)
     norm_row = jnp.sum(on_diag, axis=0, keepdims=True)

time: 97.1 us -> 97.4 us (level)
  no operation moved by 1% of the time
where the time goes in v7:
time: 97.4 us; the launch traced here: 97 us
  blocking collectives  91.9 us (94%)
  Pallas kernels  4.38 us (4%)
    all_to_all x4, blocking collectives, exchange(): lax.all_to_all(array, axes, split_axis=0, concat_axis=0, axis_index_group...  81.1 us
    all_gather x2, blocking collectives, share(): return lax.all_gather(array, 'core', axis=0, tiled=False)  10.9 us
    pallas_call x7, Pallas kernels, call(): pl.pallas_call(kernel, out_shape=out_shape, in_specs=in_specs, out_specs=...  4.38 us

profile of v7, /device:TPU:1, one launch (start us, length us, event | category | flops | bytes accessed | tf_op | source)
XLA Modules:
  0.0 97.0 jit_solution(1799912113564213354)
XLA Ops:
  0.6 1.1 %swap.1 = (f32[64,8,128]{2,1,0:T(8,128)S(1)}, f32[64,8,128]{2,1,0:T(8,128)S(1)}) custom-call(f32[64,8,128]{2,1,0:T(8,128)} %bitcast.29, f32[64,8,128]{2,1,0:T(8,128)} %bitcast.36), custom_call_target="tpu_custom_call" | custom-call | tf_op jit(solution)/shard_map/swap/pallas_call | solution.py:164
  1.7 8.7 %all-gather = f32[128,8,128]{2,1,0:T(8,128)S(1)} all-gather(f32[64,8,128]{2,1,0:T(8,128)S(1)} %get-tuple-element.28), channel_id=2, replica_groups=mesh['z'=16,'y'=4,'x'=4,'core'=2] {'core'}, dimensions={0}, use_global_device_ids=true | all-gather | bytes 786432 | tf_op jit(solution)/shard_map/swap/all_gather | solution.py:202
  10.4 56.0 %conditional.1 = ((f32[66,8,128]{2,1,0:T(8,128)S(1)}, f32[64,8,128]{2,1,0:T(8,128)S(1)})) conditional(s32[]{:T(128)} %convert_element_type.7, (f32[]{:T(128)}, f32[64,8,128]{2,1,0:T(8,128)S(1)}, f32[2,64,8,128]{3,2,1,0:T(8,128)S(1)}) %tuple.21, (f32[2,64,8,128]{3,2,1,0:T(8,128)S(1)}, f32[64,8,128]{2,1,0:T(8,128)S(1)}) %tuple.22), branch_computations={%region_0.0_spmd, %region_1.0_spmd} | conditional | flops 1 | bytes 3149880 | solution.py:244
  10.4 28.8 %all_to_all.31.slab_ref = f32[64,16,128]{2,1,0:T(8,128)S(1)} all-to-all(f32[64,16,128]{2,1,0:T(8,128)S(1)} %branch_1_fun.4), channel_id=1, replica_groups={{272,304,336,368,400,432,464,496,16,48,80,112,144,176,208,240,280,312,3..., dimensions={0} | all-to-all | bytes 1048576 | tf_op jit(solution)/shard_map/reduce_or_gather/cond/branch_1_fun/all_to_all | solution.py:196
  39.3 1.4 %branch_1_fun.5 = f32[16,2,8,128]{3,2,1,0:T(8,128)S(1)} custom-call(f32[64,16,128]{2,1,0:T(8,128)S(1)} %all_to_all.31.slab_ref), custom_call_target="tpu_custom_call" | custom-call | tf_op jit(solution)/shard_map/reduce_or_gather/cond/branch_1_fun/pallas_call | solution.py:164
  40.7 10.1 %all_to_all.32.in_ref = f32[16,2,8,128]{3,2,1,0:T(8,128)S(1)} all-to-all(f32[16,2,8,128]{3,2,1,0:T(8,128)S(1)} %branch_1_fun.5), channel_id=1, replica_groups={{20,22,16,18,28,30,24,26,4,6,0,2,12,14,8,10},{21,23,17,19,29,31,25,27,5..., dimensions={0} | all-to-all | bytes 262144 | tf_op jit(solution)/shard_map/reduce_or_gather/cond/branch_1_fun/all_to_all | solution.py:196
  50.8 15.5 %all_to_all.33.in_ref = f32[16,2,8,128]{3,2,1,0:T(8,128)S(1)} all-to-all(f32[16,2,8,128]{3,2,1,0:T(8,128)S(1)} %branch_1_fun.6), channel_id=1, replica_groups={{256,288,320,352,384,416,448,480,0,32,64,96,128,160,192,224},{257,289,3..., dimensions={0} | all-to-all | bytes 262144 | tf_op jit(solution)/shard_map/reduce_or_gather/cond/branch_1_fun/all_to_all | solution.py:196
  66.4 2.2 %all-gather.1 = f32[132,8,128]{2,1,0:T(8,128)S(1)} all-gather(f32[66,8,128]{2,1,0:T(8,128)S(1)} %get-tuple-element.29), channel_id=3, replica_groups=mesh['z'=16,'y'=4,'x'=4,'core'=2] {'core'}, dimensions={0}, use_global_device_ids=true | all-gather | bytes 811008 | tf_op jit(solution)/shard_map/reduce_or_gather/all_gather | solution.py:202
  68.6 0.0 copy-start.2
  68.6 0.7 mix.1
  69.3 0.0 copy-start
  69.4 0.0 copy-start.1
  69.4 26.6 %all_to_all.34 = f32[64,8,128]{2,1,0:T(8,128)S(1)} all-to-all(f32[64,8,128]{2,1,0:T(8,128)S(1)} %mix.1), channel_id=1, replica_groups={{272,304,336,368,400,432,464,496,16,48,80,112,144,176,208,240,280,312,3..., dimensions={0} | all-to-all | bytes 524288 | tf_op jit(solution)/shard_map/return_slab/all_to_all | solution.py:196
  96.0 0.0 copy-done.2
  96.0 0.0 copy-done
  96.0 0.0 copy-done.1
  96.0 1.1 %adam.1 = (f32[32,2048]{1,0:T(8,128)}, f32[32,2048]{1,0:T(8,128)}, f32[32,2048]{1,0:T(8,128)}, f32[32,2048]{1,0:T(8,128)}) custom-call(f32[32,2048]{1,0:T(8,128)S(1)} %bitcast.30, f32[32,2048]{1,0:T(8,128)S(1)} %bitcast.32, f32[32,2048]{1,0:T(8,128)S(1)} %bitcast.33, f32[32,2048]{1,0:T(8,128)S(1)} %bitcast.31), custom_call_target="tpu_custom_call" | custom-call | tf_op jit(solution)/shard_map/adam/pallas_call | solution.py:164
  (5 shorter events, 0.1 us)
Async XLA Ops:
  68.6 27.4 %copy-start.2 = (f32[1,32,2048]{2,1,0:T(8,128)S(1)}, f32[1,32,2048]{2,1,0:T(8,128)}, u32[]{:S(2)}) copy-start(f32[1,32,2048]{2,1,0:T(8,128)} %param.10) | copy-start | bytes 786436
  69.3 26.6 %copy-start = (f32[1,32,2048]{2,1,0:T(8,128)S(1)}, f32[1,32,2048]{2,1,0:T(8,128)}, u32[]{:S(2)}) copy-start(f32[1,32,2048]{2,1,0:T(8,128)} %param.7) | copy-start | bytes 786436
  69.4 26.6 %copy-start.1 = (f32[1,32,2048]{2,1,0:T(8,128)S(1)}, f32[1,32,2048]{2,1,0:T(8,128)}, u32[]{:S(2)}) copy-start(f32[1,32,2048]{2,1,0:T(8,128)} %param.9) | copy-start | bytes 786436

commit v8 on v7

--- a/solution.py
+++ b/solution.py
@@ -38,7 +38,8 @@
 
 def pack_kernel(slab_ref, out_ref):
     x = jnp.concatenate([slab_ref[:, s, :] for s in range(2 * SUB)], axis=1)
-    gram = dot(x, jnp.concatenate([x, x], axis=0), ((1,), (1,)))
+    gram = dot(x, x, ((1,), (1,)))
+    gram = jnp.concatenate([gram, gram], axis=1)
     lane = lax.rem(iota((COUNT, LANE), 1), COUNT)
     on_diag = jnp.where(lane == iota((COUNT, LANE), 0), gram, 0.0)
     norm_row = jnp.sum(on_diag, axis=0, keepdims=True)

time: 97.4 us -> 97.1 us (level)
  no operation moved by 1% of the time
where the time goes in v8:
time: 97.1 us; the launch traced here: 96.8 us
  blocking collectives  92.1 us (95%)
  Pallas kernels  3.92 us (4%)
    all_to_all x4, blocking collectives, exchange(): lax.all_to_all(array, axes, split_axis=0, concat_axis=0, axis_index_group...  81.2 us
    all_gather x2, blocking collectives, share(): return lax.all_gather(array, 'core', axis=0, tiled=False)  10.9 us
    pallas_call x7, Pallas kernels, call(): pl.pallas_call(kernel, out_shape=out_shape, in_specs=in_specs, out_specs=...  3.92 us

profile of v8, /device:TPU:1, one launch (start us, length us, event | category | flops | bytes accessed | tf_op | source)
XLA Modules:
  0.0 96.8 jit_solution(7810777877258430295)
XLA Ops:
  0.6 1.1 %swap.1 = (f32[64,8,128]{2,1,0:T(8,128)S(1)}, f32[64,8,128]{2,1,0:T(8,128)S(1)}) custom-call(f32[64,8,128]{2,1,0:T(8,128)} %bitcast.29, f32[64,8,128]{2,1,0:T(8,128)} %bitcast.36), custom_call_target="tpu_custom_call" | custom-call | tf_op jit(solution)/shard_map/swap/pallas_call | solution.py:165
  1.7 8.7 %all-gather = f32[128,8,128]{2,1,0:T(8,128)S(1)} all-gather(f32[64,8,128]{2,1,0:T(8,128)S(1)} %get-tuple-element.28), channel_id=2, replica_groups=mesh['z'=16,'y'=4,'x'=4,'core'=2] {'core'}, dimensions={0}, use_global_device_ids=true | all-gather | bytes 786432 | tf_op jit(solution)/shard_map/swap/all_gather | solution.py:203
  10.4 55.6 %conditional.1 = ((f32[66,8,128]{2,1,0:T(8,128)S(1)}, f32[64,8,128]{2,1,0:T(8,128)S(1)})) conditional(s32[]{:T(128)} %convert_element_type.7, (f32[]{:T(128)}, f32[64,8,128]{2,1,0:T(8,128)S(1)}, f32[2,64,8,128]{3,2,1,0:T(8,128)S(1)}) %tuple.21, (f32[2,64,8,128]{3,2,1,0:T(8,128)S(1)}, f32[64,8,128]{2,1,0:T(8,128)S(1)}) %tuple.22), branch_computations={%region_0.0_spmd, %region_1.0_spmd} | conditional | flops 1 | bytes 3149880 | solution.py:245
  10.4 28.8 %all_to_all.31.slab_ref = f32[64,16,128]{2,1,0:T(8,128)S(1)} all-to-all(f32[64,16,128]{2,1,0:T(8,128)S(1)} %branch_1_fun.4), channel_id=1, replica_groups={{272,304,336,368,400,432,464,496,16,48,80,112,144,176,208,240,280,312,3..., dimensions={0} | all-to-all | bytes 1048576 | tf_op jit(solution)/shard_map/reduce_or_gather/cond/branch_1_fun/all_to_all | solution.py:197
  39.3 1.0 branch_1_fun.5
  40.3 10.1 %all_to_all.32.in_ref = f32[16,2,8,128]{3,2,1,0:T(8,128)S(1)} all-to-all(f32[16,2,8,128]{3,2,1,0:T(8,128)S(1)} %branch_1_fun.5), channel_id=1, replica_groups={{20,22,16,18,28,30,24,26,4,6,0,2,12,14,8,10},{21,23,17,19,29,31,25,27,5..., dimensions={0} | all-to-all | bytes 262144 | tf_op jit(solution)/shard_map/reduce_or_gather/cond/branch_1_fun/all_to_all | solution.py:197
  50.4 15.5 %all_to_all.33.in_ref = f32[16,2,8,128]{3,2,1,0:T(8,128)S(1)} all-to-all(f32[16,2,8,128]{3,2,1,0:T(8,128)S(1)} %branch_1_fun.6), channel_id=1, replica_groups={{256,288,320,352,384,416,448,480,0,32,64,96,128,160,192,224},{257,289,3..., dimensions={0} | all-to-all | bytes 262144 | tf_op jit(solution)/shard_map/reduce_or_gather/cond/branch_1_fun/all_to_all | solution.py:197
  65.9 2.2 %all-gather.1 = f32[132,8,128]{2,1,0:T(8,128)S(1)} all-gather(f32[66,8,128]{2,1,0:T(8,128)S(1)} %get-tuple-element.29), channel_id=3, replica_groups=mesh['z'=16,'y'=4,'x'=4,'core'=2] {'core'}, dimensions={0}, use_global_device_ids=true | all-gather | bytes 811008 | tf_op jit(solution)/shard_map/reduce_or_gather/all_gather | solution.py:203
  68.1 0.0 copy-start.2
  68.1 0.7 mix.1
  68.9 0.0 copy-start
  68.9 0.0 copy-start.1
  68.9 26.8 %all_to_all.34 = f32[64,8,128]{2,1,0:T(8,128)S(1)} all-to-all(f32[64,8,128]{2,1,0:T(8,128)S(1)} %mix.1), channel_id=1, replica_groups={{272,304,336,368,400,432,464,496,16,48,80,112,144,176,208,240,280,312,3..., dimensions={0} | all-to-all | bytes 524288 | tf_op jit(solution)/shard_map/return_slab/all_to_all | solution.py:197
  95.7 0.0 copy-done.2
  95.7 0.0 copy-done
  95.7 0.0 copy-done.1
  95.7 1.1 %adam.1 = (f32[32,2048]{1,0:T(8,128)}, f32[32,2048]{1,0:T(8,128)}, f32[32,2048]{1,0:T(8,128)}, f32[32,2048]{1,0:T(8,128)}) custom-call(f32[32,2048]{1,0:T(8,128)S(1)} %bitcast.30, f32[32,2048]{1,0:T(8,128)S(1)} %bitcast.32, f32[32,2048]{1,0:T(8,128)S(1)} %bitcast.33, f32[32,2048]{1,0:T(8,128)S(1)} %bitcast.31), custom_call_target="tpu_custom_call" | custom-call | tf_op jit(solution)/shard_map/adam/pallas_call | solution.py:165
  (5 shorter events, 0.1 us)
Async XLA Ops:
  68.1 27.6 %copy-start.2 = (f32[1,32,2048]{2,1,0:T(8,128)S(1)}, f32[1,32,2048]{2,1,0:T(8,128)}, u32[]{:S(2)}) copy-start(f32[1,32,2048]{2,1,0:T(8,128)} %param.10) | copy-start | bytes 786436
  68.9 26.8 %copy-start = (f32[1,32,2048]{2,1,0:T(8,128)S(1)}, f32[1,32,2048]{2,1,0:T(8,128)}, u32[]{:S(2)}) copy-start(f32[1,32,2048]{2,1,0:T(8,128)} %param.7) | copy-start | bytes 786436
  68.9 26.8 %copy-start.1 = (f32[1,32,2048]{2,1,0:T(8,128)S(1)}, f32[1,32,2048]{2,1,0:T(8,128)}, u32[]{:S(2)}) copy-start(f32[1,32,2048]{2,1,0:T(8,128)} %param.9) | copy-start | bytes 786436

commit v9 on v8

--- a/solution.py
+++ b/solution.py
@@ -17,7 +17,7 @@
 COUNT = 64
 HALF = COUNT // 2
 SUB, LANE = 8, 128
-CHUNKS = 4
+CHUNKS = 2
 PACK = 16
 PACKED = PACK // SUB
 
@@ -142,9 +142,9 @@
         second = beta_two * v_ref[part] + (1.0 - beta_two) * direction * direction
         out_m[part] = first
         out_v[part] = second
-        first_hat = first / (1.0 - beta_one**ADAM_STEP)
-        second_hat = second / (1.0 - beta_two**ADAM_STEP)
-        out_x[part] = x_ref[part] + learn_rate * first_hat / (jnp.sqrt(second_hat) + adam_eps)
+        step = first * (learn_rate / (1.0 - beta_one**ADAM_STEP))
+        second_hat = second * (1.0 / (1.0 - beta_two**ADAM_STEP))
+        out_x[part] = x_ref[part] + step / (jnp.sqrt(second_hat) + adam_eps)
         for i, (src, dst) in enumerate(((out_m, new_m), (out_v, new_v), (out_x, new_x))):
             copy = pltpu.make_async_copy(src.at[part], dst.at[part], sems.at[1 + 3 * k + i])
             copy.start()

time: 97.1 us -> 97.1 us (level)
  no operation moved by 1% of the time
where the time goes in v9:
time: 97.1 us; the launch traced here: 96.7 us
  blocking collectives  92.1 us (95%)
  Pallas kernels  3.87 us (4%)
    all_to_all x4, blocking collectives, exchange(): lax.all_to_all(array, axes, split_axis=0, concat_axis=0, axis_index_group...  81.2 us
    all_gather x2, blocking collectives, share(): return lax.all_gather(array, 'core', axis=0, tiled=False)  10.9 us
    pallas_call x7, Pallas kernels, call(): pl.pallas_call(kernel, out_shape=out_shape, in_specs=in_specs, out_specs=...  3.87 us

profile of v9, /device:TPU:1, one launch (start us, length us, event | category | flops | bytes accessed | tf_op | source)
XLA Modules:
  0.0 96.7 jit_solution(15886687439927039302)
XLA Ops:
  0.6 1.1 %swap.1 = (f32[64,8,128]{2,1,0:T(8,128)S(1)}, f32[64,8,128]{2,1,0:T(8,128)S(1)}) custom-call(f32[64,8,128]{2,1,0:T(8,128)} %bitcast.29, f32[64,8,128]{2,1,0:T(8,128)} %bitcast.36), custom_call_target="tpu_custom_call" | custom-call | tf_op jit(solution)/shard_map/swap/pallas_call | solution.py:165
  1.7 8.7 %all-gather = f32[128,8,128]{2,1,0:T(8,128)S(1)} all-gather(f32[64,8,128]{2,1,0:T(8,128)S(1)} %get-tuple-element.28), channel_id=2, replica_groups=mesh['z'=16,'y'=4,'x'=4,'core'=2] {'core'}, dimensions={0}, use_global_device_ids=true | all-gather | bytes 786432 | tf_op jit(solution)/shard_map/swap/all_gather | solution.py:203
  10.4 55.6 %conditional.1 = ((f32[66,8,128]{2,1,0:T(8,128)S(1)}, f32[64,8,128]{2,1,0:T(8,128)S(1)})) conditional(s32[]{:T(128)} %convert_element_type.7, (f32[]{:T(128)}, f32[64,8,128]{2,1,0:T(8,128)S(1)}, f32[2,64,8,128]{3,2,1,0:T(8,128)S(1)}) %tuple.21, (f32[2,64,8,128]{3,2,1,0:T(8,128)S(1)}, f32[64,8,128]{2,1,0:T(8,128)S(1)}) %tuple.22), branch_computations={%region_0.0_spmd, %region_1.0_spmd} | conditional | flops 1 | bytes 3149880 | solution.py:245
  10.4 28.8 %all_to_all.31.slab_ref = f32[64,16,128]{2,1,0:T(8,128)S(1)} all-to-all(f32[64,16,128]{2,1,0:T(8,128)S(1)} %branch_1_fun.4), channel_id=1, replica_groups={{272,304,336,368,400,432,464,496,16,48,80,112,144,176,208,240,280,312,3..., dimensions={0} | all-to-all | bytes 1048576 | tf_op jit(solution)/shard_map/reduce_or_gather/cond/branch_1_fun/all_to_all | solution.py:197
  39.3 1.0 branch_1_fun.5
  40.3 10.1 %all_to_all.32.in_ref = f32[16,2,8,128]{3,2,1,0:T(8,128)S(1)} all-to-all(f32[16,2,8,128]{3,2,1,0:T(8,128)S(1)} %branch_1_fun.5), channel_id=1, replica_groups={{20,22,16,18,28,30,24,26,4,6,0,2,12,14,8,10},{21,23,17,19,29,31,25,27,5..., dimensions={0} | all-to-all | bytes 262144 | tf_op jit(solution)/shard_map/reduce_or_gather/cond/branch_1_fun/all_to_all | solution.py:197
  50.4 15.5 %all_to_all.33.in_ref = f32[16,2,8,128]{3,2,1,0:T(8,128)S(1)} all-to-all(f32[16,2,8,128]{3,2,1,0:T(8,128)S(1)} %branch_1_fun.6), channel_id=1, replica_groups={{256,288,320,352,384,416,448,480,0,32,64,96,128,160,192,224},{257,289,3..., dimensions={0} | all-to-all | bytes 262144 | tf_op jit(solution)/shard_map/reduce_or_gather/cond/branch_1_fun/all_to_all | solution.py:197
  65.9 2.2 %all-gather.1 = f32[132,8,128]{2,1,0:T(8,128)S(1)} all-gather(f32[66,8,128]{2,1,0:T(8,128)S(1)} %get-tuple-element.29), channel_id=3, replica_groups=mesh['z'=16,'y'=4,'x'=4,'core'=2] {'core'}, dimensions={0}, use_global_device_ids=true | all-gather | bytes 811008 | tf_op jit(solution)/shard_map/reduce_or_gather/all_gather | solution.py:203
  68.1 0.0 copy-start.2
  68.1 0.7 mix.1
  68.9 0.0 copy-start
  68.9 0.0 copy-start.1
  68.9 26.8 %all_to_all.34 = f32[64,8,128]{2,1,0:T(8,128)S(1)} all-to-all(f32[64,8,128]{2,1,0:T(8,128)S(1)} %mix.1), channel_id=1, replica_groups={{272,304,336,368,400,432,464,496,16,48,80,112,144,176,208,240,280,312,3..., dimensions={0} | all-to-all | bytes 524288 | tf_op jit(solution)/shard_map/return_slab/all_to_all | solution.py:197
  95.7 0.0 copy-done.2
  95.7 0.0 copy-done
  95.7 0.0 copy-done.1
  95.7 1.0 %adam.1 = (f32[32,2048]{1,0:T(8,128)}, f32[32,2048]{1,0:T(8,128)}, f32[32,2048]{1,0:T(8,128)}, f32[32,2048]{1,0:T(8,128)}) custom-call(f32[32,2048]{1,0:T(8,128)S(1)} %bitcast.30, f32[32,2048]{1,0:T(8,128)S(1)} %bitcast.32, f32[32,2048]{1,0:T(8,128)S(1)} %bitcast.33, f32[32,2048]{1,0:T(8,128)S(1)} %bitcast.31), custom_call_target="tpu_custom_call" | custom-call | tf_op jit(solution)/shard_map/adam/pallas_call | solution.py:165
  (5 shorter events, 0.1 us)
Async XLA Ops:
  68.1 27.6 %copy-start.2 = (f32[1,32,2048]{2,1,0:T(8,128)S(1)}, f32[1,32,2048]{2,1,0:T(8,128)}, u32[]{:S(2)}) copy-start(f32[1,32,2048]{2,1,0:T(8,128)} %param.10) | copy-start | bytes 786436
  68.9 26.8 %copy-start = (f32[1,32,2048]{2,1,0:T(8,128)S(1)}, f32[1,32,2048]{2,1,0:T(8,128)}, u32[]{:S(2)}) copy-start(f32[1,32,2048]{2,1,0:T(8,128)} %param.7) | copy-start | bytes 786436
  68.9 26.8 %copy-start.1 = (f32[1,32,2048]{2,1,0:T(8,128)S(1)}, f32[1,32,2048]{2,1,0:T(8,128)}, u32[]{:S(2)}) copy-start(f32[1,32,2048]{2,1,0:T(8,128)} %param.9) | copy-start | bytes 786436
